TPU v7x, 32 devices: a whole 2x2x4 slice. The times are simulated.
32 devices in a mesh: row: 8 (over y, x, core), col: 4 (over z).
Axes of the slice: x: 2, y: 2, z: 4, core: 2. Of those that a mesh axis runs over, the one named last changes fastest.
Arguments:
- parent_sigma: float32 [4, 8, 128, 8, 4, 128], P(None, 'row', None, None, 'col'), as said below
- slot_tile: int32 [8, 2], replicated, may hold values from 0 to 3, as said below
- slot_count: int32 [8], replicated, may hold values from 1 to 2, as said below
- panel: float32 [8, 2, 128, 1024], P('row'), may hold values from -0.25 to 0.25
- sep_factor: float32 [1024, 1024], P('row'), as said below
Outputs:
- sigma_update: float32 [8, 2, 128, 1024], P('row')
- sigma_sep: float32 [1024, 1024], P('row')
Inputs may be any that keep to these rules, and one draw needn't show every extreme that they name: `parent_sigma`: symmetric when viewed as a [4096, 4096] matrix. `slot_tile`: the slots of one grid row name distinct tiles in increasing order. `slot_count`: every grid row has a live slot; some grid row has all 2 slots live. `sep_factor`: lower triangular with diagonal entries from 1.5 to 3.
All inputs are finite; a program needn't handle non-finite values.
Results may differ from a plain program's by a relative error of at most 0.00024.
Values sent between devices are 32-bit elements; how exact they have to be, the bound alone decides.
A program may use at most 64 MiB of HBM per device.

v0:
```python
import jax
import jax.numpy as jnp
from jax import lax
from jax.sharding import PartitionSpec as P


def broadcast(shard, axis, root):
    mine = lax.axis_index(axis) == root
    return lax.psum(jnp.where(mine, shard, jnp.zeros_like(shard)), axis)


def exact_dot(left, right):
    return jnp.dot(left, right, precision=lax.Precision.HIGHEST, preferred_element_type=jnp.float32)


def lower_inverse(triangle):
    identity = jnp.eye(triangle.shape[0], dtype=jnp.float32)
    return jax.scipy.linalg.solve_triangular(triangle, identity, lower=True)


def combine_owners(owner_blocks, far_panels):
    partial_sum = exact_dot(owner_blocks[0], far_panels[0])
    partial_sum = partial_sum + exact_dot(owner_blocks[1], far_panels[1])
    return partial_sum


def column_total(partial_sum):
    return lax.psum(partial_sum, "col")


def row_total(stacked):
    return lax.psum(stacked, "row")


def on_device(parent_sigma, slot_tile, slot_count, panel, sep_factor):
    n_row = lax.axis_size("row")
    n_col = lax.axis_size("col")
    owner_ratio = n_row // n_col
    my_row = lax.axis_index("row")
    my_col = lax.axis_index("col")
    parent_rows = parent_sigma.shape[0]
    tile_size = parent_sigma.shape[2]
    parent_cols = parent_sigma.shape[3]
    slot_cap = panel.shape[1]
    sep_width = panel.shape[3]
    block_width = sep_width // 2
    local_sigma = parent_sigma.reshape(parent_rows, tile_size, parent_cols, tile_size)
    factor = lax.all_gather(sep_factor, "row", axis=0, tiled=True)
    first_inv = lower_inverse(factor[:block_width, :block_width])
    last_inv = lower_inverse(factor[block_width:, block_width:])
    coupling = exact_dot(factor[block_width:, :block_width], first_inv)
    live_slots = (jnp.arange(slot_cap, dtype=jnp.int32) < slot_count[my_row]).astype(jnp.float32)
    live_rows = jnp.repeat(live_slots, tile_size)[:, None]
    strips = panel.reshape(slot_cap * tile_size, sep_width) * live_rows
    first_u = exact_dot(strips[:, :block_width], first_inv)
    last_u = exact_dot(strips[:, block_width:], last_inv)
    own_block = jnp.take(local_sigma, slot_tile[my_row], axis=0)
    owner_blocks = []
    for owner_step in range(owner_ratio):
        columns = slot_tile[my_col + n_col * owner_step] * owner_ratio + owner_step
        picked = jnp.take(own_block, columns, axis=2)
        owner_blocks.append(picked.reshape(slot_cap * tile_size, slot_cap * tile_size))
    last_far = [
        broadcast(last_u, "row", my_col + n_col * owner_step) for owner_step in range(owner_ratio)
    ]
    last_partial = combine_owners(owner_blocks, last_far)
    last_y_part = column_total(last_partial) * live_rows
    inner_last = exact_dot(last_u.T, last_y_part)
    cross_part = -exact_dot(first_u.T, last_y_part)
    last_sums = row_total(jnp.stack([inner_last, cross_part]))
    sigma_last = exact_dot(last_inv.T, last_inv) + last_sums[0]
    cross_full = last_sums[1]
    first_far = [
        broadcast(first_u, "row", my_col + n_col * owner_step) for owner_step in range(owner_ratio)
    ]
    first_partial = combine_owners(owner_blocks, first_far)
    sigma_cross = exact_dot(sigma_last, coupling) + cross_full.T
    first_y = (column_total(first_partial) - exact_dot(last_y_part, coupling)) * live_rows
    first_sums = row_total(jnp.stack([exact_dot(first_u.T, first_y)]))
    sigma_first = (
        exact_dot(first_inv.T, first_inv) + first_sums[0] + exact_dot(coupling.T, sigma_cross)
    )
    update_block = -jnp.concatenate([first_y, last_y_part], axis=1)
    upper_rows = jnp.concatenate([sigma_first, -sigma_cross.T], axis=1)
    lower_rows = jnp.concatenate([-sigma_cross, sigma_last], axis=1)
    whole_sep = jnp.concatenate([upper_rows, lower_rows], axis=0)
    sep_rows = sep_width // n_row
    return (
        update_block.reshape(1, slot_cap, tile_size, sep_width),
        lax.dynamic_slice_in_dim(whole_sep, my_row * sep_rows, sep_rows, 0),
    )


def solution(mesh):
    placed = (
        P(None, "row", None, None, "col", None),
        P(),
        P(),
        P("row", None, None, None),
        P("row", None),
    )
    return jax.shard_map(
        on_device,
        mesh=mesh,
        in_specs=placed,
        out_specs=(P("row", None, None, None), P("row", None)),
        check_vma=False,
    )
```

profile of v0, /device:TPU:0, one launch (start us, length us, event | category | flops | bytes accessed | tf_op | source)
XLA Modules:
  0.0 401.1 jit_solution(17421633693418295334)
XLA Ops:
  7.2 0.7 all-gather.2.cloned.1.call-update
  8.0 1.2 dynamic_slice.17
  9.2 1.0 fusion.61
  10.3 0.6 gather_fusion
  11.0 1.2 copy.17
  12.3 0.6 compare_convert_fusion
  13.1 1.1 bitcast_multiply_fusion
  14.3 35.1 %all-gather.2.cloned.1.call-done = f32[1024,1024]{1,0:T(8,128)} async-done(((f32[128,1024]{1,0:T(8,128)}), f32[1024,1024]{1,0:T(8,128)}) %all-gather.2.cloned.1.call-update) | async-done | bytes 4194320 | tf_op jit(solution)/shard_map/all_gather | solution.py:48
  49.4 3.1 slice_select_fusion.1
  52.5 11.3 %while.4 = (s32[]{:T(128)}, f32[512,512]{1,0:T(8,128)}, s32[4,2]{0,1:T(2,128)S(1)}, f32[4,128,128]{2,1,0:T(8,128)S(1)}, s32[]{:T(128)}) while((s32[]{:T(128)}, f32[512,512]{1,0:T(8,128)}, s32[4,2]{0,1:T(2,128)S(1)}, f32[4,128,128]{2,1,0:T(8,128)S(1)}, s32[]{:T(128)}) %tuple.56), condition=%wide.while_cond, body=%wide.while_body.sunk | while | flops 2 | bytes 131189 | solution.py:18
  52.6 0.6 fusion.100
  53.2 2.2 bitcast_dynamic-update-slice_fusion.4
  55.4 0.6 fusion.100
  56.0 2.2 bitcast_dynamic-update-slice_fusion.4
  58.3 0.6 fusion.100
  58.8 2.2 bitcast_dynamic-update-slice_fusion.4
  61.1 0.6 fusion.100
  61.7 2.1 bitcast_dynamic-update-slice_fusion.4
  63.8 39.9 %custom-call.4 = f32[4,128,128]{1,2,0:T(8,128)} custom-call(f32[4,128,128]{2,1,0:T(8,128)S(1)} %get-tuple-element.18), custom_call_target="InvertDiagBlocksLowerTriangular" | custom-call | tf_op jit(solution)/shard_map/jit(_solve_triangular)/triangular_solve | solution.py:18
  103.7 10.9 %while.5 = (s32[]{:T(128)}, f32[512,512]{1,0:T(8,128)}, s32[4,2]{0,1:T(2,128)S(1)}, f32[4,128,128]{2,1,0:T(8,128)S(1)}, s32[]{:T(128)}) while((s32[]{:T(128)}, f32[512,512]{1,0:T(8,128)}, s32[4,2]{0,1:T(2,128)S(1)}, f32[4,128,128]{2,1,0:T(8,128)S(1)}, s32[]{:T(128)}) %tuple.70), condition=%wide.while_cond.clone, body=%wide.while_body.clone.sunk | while | flops 2 | bytes 131189 | solution.py:18
  104.4 2.1 bitcast_dynamic-update-slice_fusion.5
  107.1 2.1 bitcast_dynamic-update-slice_fusion.5
  109.8 2.1 bitcast_dynamic-update-slice_fusion.5
  112.6 2.1 bitcast_dynamic-update-slice_fusion.5
  114.6 39.9 %custom-call.5 = f32[4,128,128]{1,2,0:T(8,128)} custom-call(f32[4,128,128]{2,1,0:T(8,128)S(1)} %get-tuple-element.19), custom_call_target="InvertDiagBlocksLowerTriangular" | custom-call | tf_op jit(solution)/shard_map/jit(_solve_triangular)/triangular_solve | solution.py:18
  154.6 1.3 fusion.42
  155.9 1.3 fusion.40
  157.2 1.3 convolution_subtract_fusion.2
  158.4 1.3 fusion.51
  159.7 1.4 convolution_subtract_fusion.1
  161.6 1.7 convolution_subtract_fusion.5
  163.7 1.3 convolution_subtract_fusion.4
  165.4 1.4 convolution_subtract_fusion.3
  167.3 1.7 convolution_subtract_fusion.6
  169.4 2.2 broadcast_select_fusion.3
  171.7 2.2 broadcast_select_fusion.1
  174.2 1.3 gather_fusion.2
  175.5 1.3 gather_fusion.1
  176.8 1.0 select_bitcast_fusion
  178.0 1.0 select_bitcast_fusion.1
  179.3 56.6 %all-reduce.9.cloned.1.call-done = (f32[256,512]{1,0:T(8,128)}, f32[256,512]{1,0:T(8,128)}, f32[256,512]{1,0:T(8,128)}, f32[256,512]{1,0:T(8,128)}) async-done(((f32[256,512]{1,0:T(8,128)}, f32[256,512]{1,0:T(8,128)}, f32[256,512]{1,0:T(8,128)}, f32[256,512]{1,0:T(8,128)}), (f32[256,512]{1,0:T(8,128)}, f32[256,512]{1,0:T(8,128)}, f32[256,512]{1,0:T(8,128)}, ...) | async-done | bytes 2097168 | tf_op jit(solution)/shard_map/psum | solution.py:9
  235.9 1.7 fusion.32
  237.6 1.7 fusion.34
  239.3 1.4 convolution_add_fusion.3
  240.7 1.4 convolution_add_fusion.4
  242.2 4.9 %fusion.2 = f32[512,512]{1,0:T(8,128)S(1)} fusion(f32[1024,1024]{1,0:T(8,128)} %all-gather.2.cloned.1.call-done, f32[128,512]{1,0:T(8,128)} %copy-done.13, f32[128,512]{1,0:T(8,128)} %copy-done.10, f32[128,512]{1,0:T(8,128)} %copy-done.4, f32[128,512]{1,0:T(8,128)S(1)} %fusion.42), kind=kOutput, calls=%fused_computation.29 | convolution fusion | flops 1611399168 | bytes 3145728 | tf_op jit(solution)/shard_map/dot_general | solution.py:13
  247.2 46.7 %all-reduce.11.cloned.1.call-done = (f32[256,512]{1,0:T(8,128)}, f32[256,512]{1,0:T(8,128)}) async-done(((f32[256,512]{1,0:T(8,128)}, f32[256,512]{1,0:T(8,128)}), (f32[256,512]{1,0:T(8,128)}, f32[256,512]{1,0:T(8,128)})) %all-reduce.11.cloned.1.call-update) | async-done | bytes 1048592 | tf_op jit(solution)/shard_map/psum | solution.py:28
  293.9 1.2 broadcast_multiply_fusion
  295.1 2.3 convolution_bitcast_fusion
  297.4 1.1 fusion
  298.5 1.1 fusion.1
  299.6 0.8 copy-done.11
  300.4 2.1 fusion.74
  302.4 1.5 pad_maximum_fusion
  304.0 2.3 maximum_negate_fusion
  306.2 66.9 %all-reduce.7.cloned.1.call-done = (f32[512,512]{0,1:T(8,128)}, f32[2,512,512]{1,2,0:T(8,128)}) async-done(((f32[512,512]{0,1:T(8,128)}, f32[2,512,512]{1,2,0:T(8,128)}), (f32[512,512]{0,1:T(8,128)}, f32[2,512,512]{1,2,0:T(8,128)})) %all-reduce.7.cloned.1.call-update) | async-done | bytes 3145744 | tf_op jit(solution)/shard_map/psum | solution.py:32
  373.1 3.8 convolution_add_fusion.2
  377.0 1.9 convolution_add_fusion.1
  379.1 4.5 %fusion.4 = (f32[512,512]{0,1:T(8,128)}, f32[512,512]{1,0:T(8,128)S(1)}) fusion(f32[2,512,512]{1,2,0:T(8,128)S(1)} %copy-done.7, f32[512,512]{0,1:T(8,128)S(1)} %convolution_add_fusion.1, f32[512,512]{1,0:T(8,128)S(1)} %fusion.2), kind=kOutput, calls=%fused_computation.38 | convolution fusion | flops 1611137024 | bytes 5242880 | tf_op jit(solution)/shard_map/dot_general | solution.py:13
  383.7 1.2 fusion.29
  384.9 2.9 convolution_add_fusion
  387.9 2.6 copy.24
  390.5 2.0 fusion.18
  392.5 2.0 copy.25
  (91 shorter events, 6.1 us)
Async XLA Ops:
  7.2 3.1 copy-start
  7.2 42.2 %all-gather.2.cloned.1.call-start = ((), (), s32[]{:S(2)}) async-start(), calls=%async_computation | async-start | bytes 4718592 | tf_op jit(solution)/shard_map/all_gather | solution.py:48
  7.9 228.0 %all-reduce.9.cloned.1.call-start = ((), (), s32[]{:S(2)}) async-start(), calls=%async_computation.2 | async-start | bytes 4194304 | tf_op jit(solution)/shard_map/psum | solution.py:9
  11.0 2.1 copy-start.20
  154.6 6.6 %copy-start.25 = (f32[4,128,128]{1,2,0:T(8,128)S(1)}, f32[4,128,128]{1,2,0:T(8,128)}, u32[]{:S(2)}) copy-start(f32[4,128,128]{1,2,0:T(8,128)} %custom-call.5) | copy-start | bytes 786436
  157.1 14.5 %copy-start.5 = (f32[128,512]{1,0:T(8,128)}, f32[128,512]{1,0:T(8,128)S(1)}, u32[]{:S(2)}) copy-start(f32[128,512]{1,0:T(8,128)S(1)} %fusion.40) | copy-start | bytes 786436
  159.7 12.0 %copy-start.8 = (f32[128,512]{1,0:T(8,128)}, f32[128,512]{1,0:T(8,128)S(1)}, u32[]{:S(2)}) copy-start(f32[128,512]{1,0:T(8,128)S(1)} %fusion.51) | copy-start | bytes 786436
  159.7 5.3 %copy-start.24 = (f32[4,128,128]{1,2,0:T(8,128)S(1)}, f32[4,128,128]{1,2,0:T(8,128)}, u32[]{:S(2)}) copy-start(f32[4,128,128]{1,2,0:T(8,128)} %custom-call.4) | copy-start | bytes 786436
  161.6 10.1 %copy-start.14 = (f32[128,512]{1,0:T(8,128)}, f32[128,512]{1,0:T(8,128)S(1)}, u32[]{:S(2)}) copy-start(f32[128,512]{1,0:T(8,128)S(1)} %fusion.49) | copy-start | bytes 786436
  163.7 8.0 %copy-start.17 = (f32[128,512]{1,0:T(8,128)}, f32[128,512]{1,0:T(8,128)S(1)}, u32[]{:S(2)}) copy-start(f32[128,512]{1,0:T(8,128)S(1)} %fusion.48) | copy-start | bytes 786436
  165.0 4.4 %copy-start.16 = (f32[256,1024]{1,0:T(8,128)S(1)}, f32[256,1024]{1,0:T(8,128)}, u32[]{:S(2)}) copy-start(f32[256,1024]{1,0:T(8,128)} %bitcast_multiply_fusion) | copy-start | bytes 3145732
  165.4 6.2 %copy-start.4 = (f32[128,512]{1,0:T(8,128)}, f32[128,512]{1,0:T(8,128)S(1)}, u32[]{:S(2)}) copy-start(f32[128,512]{1,0:T(8,128)S(1)} %fusion.55) | copy-start | bytes 786436
  167.3 4.4 %copy-start.10 = (f32[128,512]{1,0:T(8,128)}, f32[128,512]{1,0:T(8,128)S(1)}, u32[]{:S(2)}) copy-start(f32[128,512]{1,0:T(8,128)S(1)} %fusion.53) | copy-start | bytes 786436
  169.4 4.5 %copy-start.13 = (f32[128,512]{1,0:T(8,128)}, f32[128,512]{1,0:T(8,128)S(1)}, u32[]{:S(2)}) copy-start(f32[128,512]{1,0:T(8,128)S(1)} %fusion.52) | copy-start | bytes 786436
  171.7 2.5 copy-start.19
  174.0 119.9 %all-reduce.11.cloned.1.call-start = ((), (), s32[]{:S(2)}) async-start(), calls=%async_computation.3 | async-start | bytes 2097152 | tf_op jit(solution)/shard_map/psum | solution.py:28
  235.9 3.4 copy-start.22
  235.9 4.9 %copy-start.21 = (f32[256,512]{1,0:T(8,128)S(1)}, f32[256,512]{1,0:T(8,128)}, u32[]{:S(2)}) copy-start(f32[256,512]{1,0:T(8,128)} %get-tuple-element.50) | copy-start | bytes 1572868
  242.2 130.9 %all-reduce.7.cloned.1.call-start = ((), (), s32[]{:S(2)}) async-start(), calls=%async_computation.1 | async-start | bytes 6291456 | tf_op jit(solution)/shard_map/psum | solution.py:32
  293.9 3.5 copy-start.12
  295.1 3.4 copy-start.1
  295.1 3.4 copy-start.23
  299.6 0.8 copy-start.11
  373.1 3.8 copy-start.6
  373.1 3.8 copy-start.7
  373.1 3.8 copy-start.9
  373.1 3.8 copy-start.15
  373.1 3.8 copy-start.18
  379.1 4.6 %copy-start.2 = (f32[512,512]{0,1:T(8,128)}, f32[512,512]{0,1:T(8,128)S(1)}, u32[]{:S(2)}) copy-start(f32[512,512]{0,1:T(8,128)S(1)} %convolution_add_fusion.1) | copy-start | bytes 3145732
  387.9 2.6 copy-start.3
Sparse Core Ops, SparseCore 0:
  9.9 39.4 all-gather.1
  174.1 61.7 all-reduce.8
  242.3 51.5 all-reduce.10
  304.1 69.0 all-reduce.6
where the time goes:
time: 402 us; the launch traced here: 401 us
  waiting for transfers between devices  206 us (51%)
  other arithmetic  96.4 us (24%)
  matrix products  49.9 us (12%)
  local copies, waits for them, and re-layouts  33.8 us (8%)
  between operations  14.6 us (4%)
    another operation x4, other arithmetic, lower_inverse(): return jax.scipy.linalg.solve_triangular(triangle, identity, lower=True)  83 us
    psum x1, waiting for transfers between devices, row_total(): return lax.psum(stacked, 'row')  66.9 us
    psum x1, waiting for transfers between devices, broadcast(): return lax.psum(jnp.where(mine, shard, jnp.zeros_like(shard)), axis)  56.6 us
    psum x1, waiting for transfers between devices, column_total(): return lax.psum(partial_sum, 'col')  46.7 us
    dot_general x15, matrix products, exact_dot(): jnp.dot(left, right, precision=lax.Precision.HIGHEST, preferred_element_t...  35.3 us
    all_gather x1, waiting for transfers between devices, on_device(): factor = lax.all_gather(sep_factor, 'row', axis=0, tiled=True)  35.1 us
    another operation x27, local copies, waits for them, and re-layouts, lower_inverse(): return jax.scipy.linalg.solve_triangular(triangle, identity, lower=True)  22.1 us
    another operation x14, matrix products, lower_inverse(): return jax.scipy.linalg.solve_triangular(triangle, identity, lower=True)  14.6 us
  transfers between devices with their start and end apart: 4, of which 4 were waited for; matrix products, arithmetic and copies ran while one was open for 5% of the time, Pallas kernels for 0%

commit v1 on v0

v1 whole, which is shorter than its diff:
```python
import functools

import jax
import jax.numpy as jnp
from jax import lax
from jax.experimental import pallas as pl
from jax.experimental.pallas import tpu as pltpu
from jax.sharding import PartitionSpec as P

MESH = pl.DeviceIdType.MESH
F32 = jnp.float32
BF16 = jnp.bfloat16
VMEM_BYTES = 56 * 1024 * 1024


def halves(x):
    high = x.astype(BF16)
    return high, (x - high.astype(F32)).astype(BF16)


def dot_pieces(left, right):
    (lh, ll), (rh, rl) = left, right
    one = functools.partial(jnp.dot, preferred_element_type=F32)
    return one(lh, rh) + (one(lh, rl) + one(ll, rh))


def dot3(left, right):
    return dot_pieces(halves(left), halves(right))


def exact(left, right):
    return jnp.dot(left, right, precision=lax.Precision.HIGHEST, preferred_element_type=F32)


def partial_kernel(ratio, place, tiles, counts, sigma, panel, masked, part, picked, sems):
    slot_cap, tile, _ = panel.shape[1:]
    my_row, my_col = place[0], place[1]
    n_col = tiles.shape[0] // ratio
    copies = []
    for k in range(ratio * slot_cap):
        step, slot = divmod(k, slot_cap)
        column = tiles[my_col + n_col * step, slot] * ratio + step
        for s in range(slot_cap):
            copy = pltpu.make_async_copy(
                sigma.at[tiles[my_row, s], 0, :, column, 0, :],
                picked.at[k, pl.ds(s * tile, tile)],
                sems.at[k, s],
            )
            copy.start()
            copies.append(copy)
    for s in range(slot_cap):
        live = jnp.where(s < counts[my_row], 1.0, 0.0).astype(F32)
        masked[pl.ds(s * tile, tile), :] = panel[0, s] * live
    strips = halves(masked[...])
    for copy in copies:
        copy.wait()
    for k in range(ratio * slot_cap):
        step, slot = divmod(k, slot_cap)
        live = jnp.where(slot < counts[my_col + n_col * step], 1.0, 0.0).astype(F32)
        block = picked[k].T * live
        part[pl.ds(k * tile, tile), :] = dot_pieces(halves(block), strips)


def base_inverse(block):
    size = block.shape[0]
    row = lax.broadcasted_iota(jnp.int32, block.shape, 0)
    col = lax.broadcasted_iota(jnp.int32, block.shape, 1)
    diagonal = row == col
    inverse = jnp.where(diagonal, 1.0 / jnp.where(diagonal, block, 1.0), 0.0)
    for level in range(size.bit_length() - 1):
        row_block, col_block = row >> level, col >> level
        below = jnp.where((row_block == col_block + 1) & ((row_block & 1) == 1), block, 0.0)
        inverse = inverse - exact(inverse, exact(below, inverse))
    return inverse


def main_kernel(
    n_row, n_col, part, masked, sep, out_update, out_sep,
    pair_in, half_sum, scatter_in, chain, z_full, factor, own_rows, both, stacked, stacked_y,
    s_part, s_pair, s_half, s_in, s_own, s_full,
    pair_sem, scatter_send, scatter_recv, own_send, own_recv, far_send, far_recv, pass_send, pass_recv,
    up_send, down_send, chain_recv, give_send, give_recv,
    s_pair_sem, s_scatter_send, s_scatter_recv, s_give_send, s_give_recv,
):
    me, plane = lax.axis_index("row"), lax.axis_index("col")
    pairs = n_row // 2
    parity, mine = lax.rem(me, 2), lax.div(me, 2)
    sibling = me + 1 - 2 * parity
    width = sep.shape[1]
    sep_rows = sep.shape[0]
    front = masked.shape[0]
    chunk = part.shape[0] // n_row
    per_front = front // chunk
    half_rows = pairs * chunk
    half_width = width // 2

    def remote(src, dst, send, recv, row, col):
        return pltpu.make_async_remote_copy(
            src_ref=src, dst_ref=dst, send_sem=send, recv_sem=recv,
            device_id=(row, col), device_id_type=MESH,
        )

    barrier = pltpu.get_barrier_semaphore()
    for d in range(1, n_row):
        pl.semaphore_signal(barrier, inc=1, device_id=(lax.rem(me + d, n_row), plane), device_id_type=MESH)
    for d in range(1, n_col):
        pl.semaphore_signal(barrier, inc=1, device_id=(me, lax.rem(plane + d, n_col)), device_id_type=MESH)
    pl.semaphore_wait(barrier, n_row + n_col - 2)

    theirs = pl.ds(pl.multiple_of((1 - parity) * half_rows, 8), half_rows)
    ours = pl.ds(pl.multiple_of(parity * half_rows, 8), half_rows)
    pair = remote(part.at[theirs], pair_in, pair_sem.at[0], pair_sem.at[1], sibling, plane)
    pair.start()
    factor[pl.ds(0, half_width), pl.ds(half_width, half_width)] = jnp.zeros((half_width, half_width), F32)
    pair.wait()
    half_sum[...] = part[ours, :] + pair_in[...]
    scatters = []
    for d in range(1, pairs):
        k = lax.rem(mine + d, pairs)
        rows = pl.ds(pl.multiple_of(k * chunk, 8), chunk)
        copy = remote(
            half_sum.at[rows], scatter_in.at[d - 1], scatter_send.at[d - 1], scatter_recv.at[d - 1],
            2 * k + parity, plane,
        )
        copy.start()
        scatters.append(copy)

    own_rows[...] = sep[...]
    whole_tile = sep_rows % 128 == 0
    if whole_tile:
        diagonal = pl.ds(pl.multiple_of(me * sep_rows, 128), sep_rows)
        own_rows[:, diagonal] = base_inverse(sep[:, diagonal])
    columns = (pl.ds(0, half_width), pl.ds(half_width, half_width))

    def rows_of(q):
        return pl.ds(pl.multiple_of(q * sep_rows, 8), sep_rows)

    def each_half(q, action):
        action(0)

        @pl.when(q >= pairs)
        def _():
            action(1)

    def own_copy(h):
        return remote(
            own_rows.at[:, columns[h]], factor.at[rows_of(me), columns[h]],
            own_send.at[h], own_recv.at[h], sibling, plane,
        )

    def far_copy(d, h):
        return remote(
            own_rows.at[:, columns[h]], factor.at[rows_of(me), columns[h]],
            far_send.at[d - 1, h], far_recv.at[d - 1, h],
            2 * lax.rem(mine + d, pairs) + parity, plane,
        )

    def pass_copy(d, h):
        q = 2 * lax.rem(mine + pairs - d, pairs) + parity
        return remote(
            factor.at[rows_of(q), columns[h]], factor.at[rows_of(q), columns[h]],
            pass_send.at[d - 1, h], pass_recv.at[d - 1, h], sibling, plane,
        )

    def far_source(d):
        return 2 * lax.rem(mine + pairs - d, pairs) + parity

    def sibling_source(d):
        return 2 * lax.rem(mine + pairs - d, pairs) + 1 - parity

    def start_rows(h):
        for d in range(1, pairs):
            far_copy(d, h).start()
        own_copy(h).start()

    each_half(me, start_rows)
    factor[rows_of(me), columns[0]] = own_rows[:, columns[0]]

    @pl.when(me >= pairs)
    def _():
        factor[rows_of(me), columns[1]] = own_rows[:, columns[1]]

    total = half_sum[pl.ds(pl.multiple_of(mine * chunk, 8), chunk), :]
    for d in range(1, pairs):
        scatters[d - 1].wait()
        total = total + scatter_in[d - 1]
    chain[plane] = total
    position = parity * pairs + mine
    owner_step = lax.div(position, per_front)
    place = lax.rem(position, per_front)
    z_rows = pl.ds(pl.multiple_of(place * chunk, 8), chunk)

    def up_copy(d):
        c = plane - d
        return remote(chain.at[c], chain.at[c], up_send.at[d], chain_recv.at[c], me, plane + 1)

    def down_copy(d):
        c = plane + d
        return remote(chain.at[c], chain.at[c], down_send.at[d], chain_recv.at[c], me, plane - 1)

    def give_copy(c):
        return remote(
            chain.at[c], z_full.at[z_rows], give_send.at[c], give_recv.at[place], c + n_col * owner_step, plane
        )

    def give(c):
        owner = c + n_col * owner_step

        @pl.when(owner == me)
        def _():
            z_full[z_rows, :] = chain[c]

        @pl.when(owner != me)
        def _():
            give_copy(c).start()

    def forward_rows(d):
        def action(h):
            far_copy(d, h).wait_recv()
            pass_copy(d, h).start()

        each_half(far_source(d), action)

    for d in range(n_col):
        @pl.when(plane >= d)
        def _():
            if d:
                remote(
                    chain.at[plane - d], chain.at[plane - d], up_send.at[d], chain_recv.at[plane - d], me, plane - 1
                ).wait_recv()

            @pl.when(plane + 1 < n_col)
            def _():
                up_copy(d).start()

        @pl.when(plane + d < n_col)
        def _():
            if d:
                remote(
                    chain.at[plane + d], chain.at[plane + d], down_send.at[d], chain_recv.at[plane + d], me, plane + 1
                ).wait_recv()

            @pl.when(plane > 0)
            def _():
                down_copy(d).start()

        @pl.when(plane >= d)
        def _():
            give(plane - d)

        if d:
            @pl.when(plane + d < n_col)
            def _():
                give(plane + d)

        if 0 < d < pairs:
            forward_rows(d)
    for d in range(n_col, pairs):
        forward_rows(d)

    each_half(sibling, lambda h: own_copy(h).wait_recv())
    for d in range(1, pairs):
        each_half(sibling_source(d), lambda h: pass_copy(d, h).wait_recv())
        each_half(far_source(d), lambda h: pass_copy(d, h).wait_send())
    if not whole_tile:
        for j in range(width // 128):
            tile = pl.ds(j * 128, 128)
            factor[tile, tile] = base_inverse(factor[tile, tile])
    size = max(sep_rows, 128) if whole_tile else 128
    while size < width:
        for start in range(0, width, 2 * size):
            first, last = pl.ds(start, size), pl.ds(start + size, size)
            inner = dot3(factor[last, first], factor[first, first])
            factor[last, first] = -dot3(factor[last, last], inner)
        size *= 2

    my_step = lax.div(me, n_col)
    for j in range(per_front):
        source = my_step * per_front + j
        source_row = 2 * lax.rem(source, pairs) + lax.div(source, pairs)

        @pl.when(source_row != me)
        def _():
            rows = pl.ds(j * chunk, chunk)
            remote(
                chain.at[plane], z_full.at[rows], give_send.at[0], give_recv.at[j], sibling, plane
            ).wait_recv()

    both[pl.ds(0, front), :] = masked[...]
    both[pl.ds(front, front), :] = z_full[...]
    block = 256
    for j in range(width // block):
        depth = pl.ds(j * block, width - j * block)
        here = pl.ds(j * block, block)
        product = dot3(both[:, depth], factor[depth, here])
        stacked[pl.ds(0, front), here] = product[:front]
        out_update[:, here] = -product[front:]
    stacked[pl.ds(front, sep_rows), :] = factor[rows_of(me), :]

    s_cols = s_own.shape[1]
    repeat = n_col * s_cols // width
    my_cols = pl.ds(pl.multiple_of(lax.div(plane, repeat) * s_cols, 128), s_cols)
    stacked_y[pl.ds(0, front), :] = -out_update[:, my_cols]
    stacked_y[pl.ds(front, sep_rows), :] = stacked[pl.ds(front, sep_rows), my_cols]
    right = halves(stacked_y[...])
    split = 128 // sep_rows
    for j in range(width // 128):
        left = halves(stacked[:, pl.ds(j * 128, 128)].T)
        product = dot_pieces(left, right)
        for i in range(split):
            q = j * split + i
            s_part[q % 2, q // 2] = product[i * sep_rows:(i + 1) * sep_rows]
    s_pairing = remote(s_part.at[1 - parity], s_pair, s_pair_sem.at[0], s_pair_sem.at[1], sibling, plane)
    s_pairing.start()
    s_pairing.wait()
    s_half[...] = s_part[parity] + s_pair[...]
    scatters_s = []
    for d in range(1, pairs):
        k = lax.rem(mine + d, pairs)
        copy = remote(
            s_half.at[k], s_in.at[d - 1], s_scatter_send.at[d - 1], s_scatter_recv.at[d - 1], 2 * k + parity, plane
        )
        copy.start()
        scatters_s.append(copy)
    total = s_half[mine]
    for d in range(1, pairs):
        scatters_s[d - 1].wait()
        total = total + s_in[d - 1]
    s_own[...] = total
    s_full[:, my_cols] = total

    def s_copy(d):
        return remote(
            s_own, s_full.at[:, my_cols], s_give_send.at[d - 1], s_give_recv.at[lax.div(plane, repeat)],
            me, lax.rem(plane + d, n_col),
        )

    @pl.when(lax.rem(plane, repeat) == 0)
    def _():
        for d in range(1, n_col):
            s_copy(d).start()

    for b in range(width // s_cols):
        source = b * repeat

        @pl.when((source != plane) & (lax.div(plane, repeat) != b))
        def _():
            remote(
                s_own, s_full.at[:, pl.ds(b * s_cols, s_cols)], s_give_send.at[0], s_give_recv.at[b], me, source
            ).wait_recv()

    out_sep[...] = s_full[...]

    @pl.when(lax.rem(plane, repeat) == 0)
    def _():
        for d in range(1, n_col):
            s_copy(d).wait_send()

    def sent_rows(h):
        for d in range(1, pairs):
            far_copy(d, h).wait_send()
        own_copy(h).wait_send()

    each_half(me, sent_rows)
    for d in range(n_col):
        @pl.when((plane >= d) & (plane + 1 < n_col))
        def _():
            up_copy(d).wait_send()

        @pl.when((plane + d < n_col) & (plane > 0))
        def _():
            down_copy(d).wait_send()
    for c in range(n_col):
        @pl.when(c + n_col * owner_step != me)
        def _():
            give_copy(c).wait_send()


def on_device(parent_sigma, slot_tile, slot_count, panel, sep_factor):
    n_row = lax.axis_size("row")
    n_col = lax.axis_size("col")
    ratio = n_row // n_col
    slot_cap, tile, width = panel.shape[1:]
    front = slot_cap * tile
    sep_rows = sep_factor.shape[0]
    place = jnp.stack([lax.axis_index("row"), lax.axis_index("col")]).astype(jnp.int32)
    vmem = pl.BlockSpec(memory_space=pltpu.VMEM)
    smem = pl.BlockSpec(memory_space=pltpu.SMEM)
    masked, part = pl.pallas_call(
        functools.partial(partial_kernel, ratio),
        out_shape=(
            jax.ShapeDtypeStruct((front, width), F32),
            jax.ShapeDtypeStruct((ratio * front, width), F32),
        ),
        in_specs=[smem, smem, smem, pl.BlockSpec(memory_space=pl.ANY), vmem],
        out_specs=(vmem, vmem),
        scratch_shapes=[
            pltpu.VMEM((ratio * slot_cap, front, tile), F32),
            pltpu.SemaphoreType.DMA((ratio * slot_cap, slot_cap)),
        ],
        compiler_params=pltpu.CompilerParams(vmem_limit_bytes=VMEM_BYTES),
    )(place, slot_tile, slot_count, parent_sigma, panel)

    pairs = n_row // 2
    chunk = ratio * front // n_row
    s_cols = max(128, width // n_col)
    dma = pltpu.SemaphoreType.DMA
    update, sep = pl.pallas_call(
        functools.partial(main_kernel, n_row, n_col),
        out_shape=(
            jax.ShapeDtypeStruct((front, width), F32),
            jax.ShapeDtypeStruct((sep_rows, width), F32),
        ),
        in_specs=[vmem] * 3,
        out_specs=(vmem, vmem),
        scratch_shapes=[
            pltpu.VMEM((pairs * chunk, width), F32),
            pltpu.VMEM((pairs * chunk, width), F32),
            pltpu.VMEM((pairs - 1, chunk, width), F32),
            pltpu.VMEM((n_col, chunk, width), F32),
            pltpu.VMEM((front, width), F32),
            pltpu.VMEM((width, width), F32),
            pltpu.VMEM((sep_rows, width), F32),
            pltpu.VMEM((2 * front, width), F32),
            pltpu.VMEM((front + sep_rows, width), F32),
            pltpu.VMEM((front + sep_rows, s_cols), F32),
            pltpu.VMEM((2, pairs, sep_rows, s_cols), F32),
            pltpu.VMEM((pairs, sep_rows, s_cols), F32),
            pltpu.VMEM((pairs, sep_rows, s_cols), F32),
            pltpu.VMEM((pairs - 1, sep_rows, s_cols), F32),
            pltpu.VMEM((sep_rows, s_cols), F32),
            pltpu.VMEM((sep_rows, width), F32),
            dma((2,)), dma((pairs - 1,)), dma((pairs - 1,)), dma((2,)), dma((2,)),
            dma((pairs - 1, 2)), dma((pairs - 1, 2)), dma((pairs - 1, 2)), dma((pairs - 1, 2)),
            dma((n_col,)), dma((n_col,)), dma((n_col,)), dma((n_col,)), dma((front // chunk,)),
            dma((2,)), dma((pairs - 1,)), dma((pairs - 1,)), dma((n_col,)), dma((width // s_cols,)),
        ],
        compiler_params=pltpu.CompilerParams(
            collective_id=0, has_side_effects=True, vmem_limit_bytes=VMEM_BYTES
        ),
    )(part, masked, sep_factor)
    return update.reshape(1, slot_cap, tile, width), sep


def solution(mesh):
    placed = (
        P(None, "row", None, None, "col", None),
        P(),
        P(),
        P("row", None, None, None),
        P("row", None),
    )
    return jax.shard_map(
        on_device,
        mesh=mesh,
        in_specs=placed,
        out_specs=(P("row", None, None, None), P("row", None)),
        check_vma=False,
    )
```

time: 402 us -> 93.2 us (0.23)
  waiting for transfers between devices: 206 us -> 0 us
  other arithmetic: 96.4 us -> 0.56 us
  Pallas kernels: 0 us -> 87.1 us
  matrix products: 49.9 us -> 0 us
  local copies, waits for them, and re-layouts: 33.8 us -> 4.51 us
  between operations: 14.6 us -> 0.66 us
    psum x3 -> x0, waiting for transfers between devices: 170 us -> none  [the longest x1 66.9 us: row_total(): return lax.psum(stacked, 'row')]
    pallas_call x0 -> x2, Pallas kernels: none -> 87.1 us  [the longest x1 82.4 us: on_device(): pl.pallas_call(functools.partial(main_kernel, n_row, n_col), out_shape=(j...]
    another operation x5 -> x1, other arithmetic: 84.5 us -> 0.56 us  [on_device(): jnp.stack([lax.axis_index('row'), lax.axis_index('col')]).astype(jnp.int32)]
    dot_general x15 -> x0, matrix products: 35.3 us -> none  [exact_dot(): jnp.dot(left, right, precision=lax.Precision.HIGHEST, preferred_element_t...]
    all_gather x1 -> x0, waiting for transfers between devices: 35.1 us -> none  [on_device(): factor = lax.all_gather(sep_factor, 'row', axis=0, tiled=True)]
    another operation x27 -> x0, local copies, waits for them, and re-layouts: 22.1 us -> none  [lower_inverse(): return jax.scipy.linalg.solve_triangular(triangle, identity, lower=True)]
    another operation x14 -> x0, matrix products: 14.6 us -> none  [lower_inverse(): return jax.scipy.linalg.solve_triangular(triangle, identity, lower=True)]
  transfers between devices with their start and end apart: 4 -> 0, of which waited for: 4 -> 0; matrix products, arithmetic and copies ran while one was open for 5% -> 0% of each run, Pallas kernels for 0% -> 0%
where the time goes in v1:
time: 93.2 us; the launch traced here: 92.9 us
  Pallas kernels  87.1 us (93%)
  local copies, waits for them, and re-layouts  4.51 us (5%)
    pallas_call x1, Pallas kernels, on_device(): pl.pallas_call(functools.partial(main_kernel, n_row, n_col), out_shape=(j...  82.4 us
    pallas_call x1, Pallas kernels, on_device(): pl.pallas_call(functools.partial(partial_kernel, ratio), out_shape=(jax.S...  4.74 us
    unnamed x5, local copies, waits for them, and re-layouts  4.51 us

profile of v1, /device:TPU:0, one launch (start us, length us, event | category | flops | bytes accessed | tf_op | source)
XLA Modules:
  0.0 92.9 jit_solution(9451999365395615243)
XLA Ops:
  0.6 0.6 pad_add_fusion.place
  1.2 1.3 %copy.7.tiles = s32[8,2]{1,0:T(8,128)} copy(s32[8,2]{0,1:T(2,128)} %param.6) | data formatting | bytes 128 | tf_op args[1]
  2.5 4.7 %shard_map.68 = (f32[256,1024]{1,0:T(8,128)}, f32[512,1024]{1,0:T(8,128)}) custom-call(s32[2]{0:T(128)} %pad_add_fusion.place, s32[8,2]{1,0:T(8,128)} %copy.7.tiles, s32[8]{0:T(128)} %counts.1, f32[4,1,128,8,1,128]{5,4,3,2,1,0:T(1,128)} %sigma.1, f32[1,2,128,1024]{3,2,1,0:T(8,128)} %panel.1), custom_call_target="tpu_custom_call" | custom-call | tf_op jit(solution)/shard_map/pallas_call | solution.py:389
  7.3 82.4 %shard_map.69 = (f32[256,1024]{1,0:T(8,128)}, f32[128,1024]{1,0:T(8,128)}) custom-call(f32[512,1024]{1,0:T(8,128)} %get-tuple-element.6.part, f32[256,1024]{1,0:T(8,128)} %get-tuple-element.7.masked, f32[128,1024]{1,0:T(8,128)} %sep.1), custom_call_target="tpu_custom_call" | custom-call | tf_op jit(solution)/shard_map/pallas_call | solution.py:408
  89.7 0.0 copy-start
  89.7 2.4 %copy.10 = f32[1,2,128,1024]{3,2,1,0:T(8,128)} copy(f32[1,2,128,1024]{3,2,1,0:T(8,128)} %bitcast.3) | data formatting | bytes 2097152
  92.1 0.0 copy-done
  92.1 0.8 copy.11
Async XLA Ops:
  89.7 2.4 %copy-start = (f32[128,1024]{1,0:T(8,128)S(1)}, f32[128,1024]{1,0:T(8,128)}, u32[]{:S(2)}) copy-start(f32[128,1024]{1,0:T(8,128)} %get-tuple-element.13) | copy-start | bytes 1572868

commit v2 on v1

v2 whole, which is shorter than its diff:
```python
import functools

import jax
import jax.numpy as jnp
from jax import lax
from jax.experimental import pallas as pl
from jax.experimental.pallas import tpu as pltpu
from jax.sharding import PartitionSpec as P

MESH = pl.DeviceIdType.MESH
F32 = jnp.float32
BF16 = jnp.bfloat16
VMEM_BYTES = 56 * 1024 * 1024
VIEWS = 2


def halves(x):
    high = x.astype(BF16)
    return high, (x - high.astype(F32)).astype(BF16)


def dot_pieces(left, right):
    (lh, ll), (rh, rl) = left, right
    one = functools.partial(jnp.dot, preferred_element_type=F32)
    return one(lh, rh) + (one(lh, rl) + one(ll, rh))


def dot3(left, right):
    return dot_pieces(halves(left), halves(right))


def exact(left, right):
    return jnp.dot(left, right, precision=lax.Precision.HIGHEST, preferred_element_type=F32)


def partial_kernel(ratio, place, tiles, counts, sigma, panel, masked, part, picked, sems):
    slot_cap, tile, _ = panel.shape[1:]
    my_row, my_col = place[0], place[1]
    n_col = tiles.shape[0] // ratio
    copies = []
    for k in range(ratio * slot_cap):
        step, slot = divmod(k, slot_cap)
        column = tiles[my_col + n_col * step, slot] * ratio + step
        for s in range(slot_cap):
            copy = pltpu.make_async_copy(
                sigma.at[tiles[my_row, s], 0, :, column, 0, :],
                picked.at[k, pl.ds(s * tile, tile)],
                sems.at[k, s],
            )
            copy.start()
            copies.append(copy)
    for s in range(slot_cap):
        live = jnp.where(s < counts[my_row], 1.0, 0.0).astype(F32)
        masked[pl.ds(s * tile, tile), :] = panel[0, s] * live
    strips = halves(masked[...])
    for copy in copies:
        copy.wait()
    for k in range(ratio * slot_cap):
        step, slot = divmod(k, slot_cap)
        live = jnp.where(slot < counts[my_col + n_col * step], 1.0, 0.0).astype(F32)
        block = picked[k].T * live
        product = dot_pieces(halves(block), strips)
        views, _, _, chunk, view_width = part.shape
        for i in range(tile // chunk):
            q = k * (tile // chunk) + i
            for v in range(views):
                part[v, q % 2, q // 2] = product[
                    i * chunk:(i + 1) * chunk, v * view_width:(v + 1) * view_width
                ]


def base_inverse(block):
    size = block.shape[0]
    row = lax.broadcasted_iota(jnp.int32, block.shape, 0)
    col = lax.broadcasted_iota(jnp.int32, block.shape, 1)
    diagonal = row == col
    inverse = jnp.where(diagonal, 1.0 / jnp.where(diagonal, block, 1.0), 0.0)
    for level in range(size.bit_length() - 1):
        row_block, col_block = row >> level, col >> level
        below = jnp.where((row_block == col_block + 1) & ((row_block & 1) == 1), block, 0.0)
        inverse = inverse - exact(inverse, exact(below, inverse))
    return inverse


def main_kernel(
    n_row, n_col, part, masked, sep, out_update, out_sep,
    pair_in, half_sum, scatter_in, chain, z_full, factor, own_rows, both, stacked, stacked_y,
    s_part, s_pair, s_half, s_in, s_full,
    pair_send, pair_recv, scatter_send, scatter_recv,
    own_send, own_recv, far_send, far_recv, pass_send, pass_recv,
    up_send, down_send, chain_recv, give_send, give_recv,
    s_pair_sem, s_send, s_recv, s_up_send, s_down_send, s_chain_recv,
):
    me, plane = lax.axis_index("row"), lax.axis_index("col")
    pairs = n_row // 2
    bits = pairs.bit_length() - 1
    parity, mine = lax.rem(me, 2), lax.div(me, 2)
    sibling = me + 1 - 2 * parity
    width = sep.shape[1]
    sep_rows = sep.shape[0]
    front = masked.shape[0]
    chunk = half_sum.shape[2]
    views = half_sum.shape[0]
    view_width = width // views

    def remote(src, dst, send, recv, row, col):
        return pltpu.make_async_remote_copy(
            src_ref=src, dst_ref=dst, send_sem=send, recv_sem=recv,
            device_id=(row, col), device_id_type=MESH,
        )

    barrier = pltpu.get_barrier_semaphore()
    for d in range(1, n_row):
        pl.semaphore_signal(barrier, inc=1, device_id=(lax.rem(me + d, n_row), plane), device_id_type=MESH)
    for d in range(1, n_col):
        pl.semaphore_signal(barrier, inc=1, device_id=(me, lax.rem(plane + d, n_col)), device_id_type=MESH)
    pl.semaphore_wait(barrier, n_row + n_col - 2)

    flip = [(1 - 2 * lax.rem(lax.div(mine, 1 << b), 2)) * (1 << b) for b in range(bits)]
    order = [(1 - parity) * flip[s] + parity * flip[bits - 1 - s] for s in range(bits)]

    def moved(steps, offset):
        pair = mine
        for s in range(bits):
            if offset >> s & 1:
                pair = pair + steps[s]
        return pair

    def sums(held, landed, send, recv):
        def copy(offset):
            s = (offset & -offset).bit_length() - 1
            return remote(
                held.at[moved(order, offset)], landed.at[offset - 1], send.at[offset - 1], recv.at[offset - 1],
                2 * (mine + order[s]) + parity, plane,
            )

        def gathered(offset, s):
            total = held[moved(order, offset)]
            for t in range(s):
                copy(offset | 1 << t).wait_recv()
                total = total + landed[(offset | 1 << t) - 1]
            return total

        def phase(s):
            for offset in reversed(range(1 << s, pairs, 2 << s)):
                if s:
                    held[moved(order, offset)] = gathered(offset, s)
                copy(offset).start()

        def finish():
            return gathered(0, bits)

        def drain():
            for offset in range(1, pairs):
                copy(offset).wait_send()

        return phase, finish, drain

    def pair_copy(v):
        return remote(part.at[v, 1 - parity], pair_in.at[v], pair_send.at[v], pair_recv.at[v], sibling, plane)

    for v in range(views):
        pair_copy(v).start()
    block = 256
    for g in range(width // block - 1):
        rest = width - (g + 1) * block
        factor[pl.ds(g * block, block), pl.ds((g + 1) * block, rest)] = jnp.zeros((block, rest), F32)
    reductions = [
        sums(half_sum.at[v], scatter_in.at[v], scatter_send.at[v], scatter_recv.at[v]) for v in range(views)
    ]
    for v in range(views):
        pair_copy(v).wait_recv()
        half_sum[v] = part[v, parity] + pair_in[v]
        reductions[v][0](0)

    own_rows[...] = sep[...]
    whole_tile = sep_rows % 128 == 0
    if whole_tile:
        diagonal = pl.ds(pl.multiple_of(me * sep_rows, 128), sep_rows)
        own_rows[:, diagonal] = base_inverse(sep[:, diagonal])
    for s in range(1, bits):
        for v in range(views):
            reductions[v][0](s)

    def rows_of(q):
        return pl.ds(pl.multiple_of(q * sep_rows, 8), sep_rows)

    def by_width(q, action):
        for g in range(width // block):
            @pl.when(lax.div(q * sep_rows, block) == g)
            def _():
                action(pl.ds(0, (g + 1) * block))

    def row_block(offset):
        return 2 * moved(flip, offset) + parity

    def own_copy(cols):
        return remote(
            own_rows.at[:, cols], factor.at[rows_of(me), cols], own_send.at[0], own_recv.at[0], sibling, plane
        )

    def far_copy(offset, b, cols):
        rows = rows_of(row_block(offset))
        source = factor.at[rows, cols] if offset else own_rows.at[:, cols]
        slot = offset + (1 << b) - 1
        return remote(
            source, factor.at[rows, cols], far_send.at[slot], far_recv.at[slot],
            2 * (mine + flip[b]) + parity, plane,
        )

    def arrived(offset, cols):
        b = offset.bit_length() - 1
        rows = rows_of(row_block(offset))
        remote(
            factor.at[rows, cols], factor.at[rows, cols], far_send.at[offset - 1], far_recv.at[offset - 1],
            2 * (mine + flip[b]) + parity, plane,
        ).wait_recv()

    def pass_copy(offset, cols):
        rows = rows_of(row_block(offset))
        return remote(
            factor.at[rows, cols], factor.at[rows, cols],
            pass_send.at[offset - 1], pass_recv.at[offset - 1], sibling, plane,
        )

    def start_rows(cols):
        for b in range(bits):
            far_copy(0, b, cols).start()
        own_copy(cols).start()
        factor[rows_of(me), cols] = own_rows[:, cols]

    by_width(me, start_rows)

    def forward_rows(offset):
        def action(cols):
            arrived(offset, cols)
            for b in range(offset.bit_length(), bits):
                far_copy(offset, b, cols).start()
            pass_copy(offset, cols).start()

        by_width(row_block(offset), action)

    owner_step = lax.div(me, n_col)
    place = lax.rem(me, n_col)
    z_rows = pl.ds(pl.multiple_of(place * chunk, 8), chunk)

    def view_cols(v):
        return pl.ds(v * view_width, view_width)

    def chain_step(slots, valid, up, down, recv, d):
        below, above = plane - d, plane + d
        if d:
            @pl.when((below >= 0) & valid(below))
            def _():
                ref = slots(below)
                remote(ref, ref, up.at[d], recv.at[below], me, plane - 1).wait_recv()

        @pl.when((below >= 0) & (plane + 1 < n_col) & valid(below))
        def _():
            ref = slots(below)
            remote(ref, ref, up.at[d], recv.at[below], me, plane + 1).start()

        if d:
            @pl.when((above < n_col) & valid(above))
            def _():
                ref = slots(above)
                remote(ref, ref, down.at[d], recv.at[above], me, plane + 1).wait_recv()

        @pl.when((above < n_col) & (plane > 0) & valid(above))
        def _():
            ref = slots(above)
            remote(ref, ref, down.at[d], recv.at[above], me, plane - 1).start()

    def chain_drain(slots, valid, up, down, recv):
        for d in range(n_col):
            below, above = plane - d, plane + d

            @pl.when((below >= 0) & (plane + 1 < n_col) & valid(below))
            def _():
                ref = slots(below)
                remote(ref, ref, up.at[d], recv.at[below], me, plane + 1).wait_send()

            @pl.when((above < n_col) & (plane > 0) & valid(above))
            def _():
                ref = slots(above)
                remote(ref, ref, down.at[d], recv.at[above], me, plane - 1).wait_send()

    def always(c):
        return c >= 0

    def give_copy(v, c):
        return remote(
            chain.at[v, c], z_full.at[z_rows, view_cols(v)], give_send.at[v, c], give_recv.at[v, place],
            c + n_col * owner_step, plane,
        )

    def give(v, c):
        @pl.when(c == place)
        def _():
            z_full[z_rows, view_cols(v)] = chain[v, c]

        @pl.when(c != place)
        def _():
            give_copy(v, c).start()

    def z_chain(v):
        return functools.partial(lambda v, c: chain.at[v, c], v), always, up_send.at[v], down_send.at[v], chain_recv.at[v]

    for d in range(n_col):
        for v in range(views):
            if d == 0:
                chain[v, plane] = reductions[v][1]()
            chain_step(*z_chain(v), d)

            @pl.when(plane >= d)
            def _():
                give(v, plane - d)

            if d:
                @pl.when(plane + d < n_col)
                def _():
                    give(v, plane + d)

        if d + 1 < pairs:
            forward_rows(d + 1)
    for offset in range(n_col + 1, pairs):
        forward_rows(offset)

    by_width(sibling, lambda cols: own_copy(cols).wait_recv())
    for offset in range(1, pairs):
        by_width(row_block(offset) + 1 - 2 * parity, lambda cols: pass_copy(offset, cols).wait_recv())

        def sent(cols):
            for b in range(offset.bit_length(), bits):
                far_copy(offset, b, cols).wait_send()
            pass_copy(offset, cols).wait_send()

        by_width(row_block(offset), sent)
    if not whole_tile:
        for j in range(width // 128):
            tile = pl.ds(j * 128, 128)
            factor[tile, tile] = base_inverse(factor[tile, tile])
    size = max(sep_rows, 128) if whole_tile else 128
    while size < width:
        for start in range(0, width, 2 * size):
            first, last = pl.ds(start, size), pl.ds(start + size, size)
            inner = dot3(factor[last, first], factor[first, first])
            factor[last, first] = -dot3(factor[last, last], inner)
        size *= 2

    for j in range(n_col):
        @pl.when(j != place)
        def _():
            for v in range(views):
                remote(
                    chain.at[v, plane], z_full.at[pl.ds(j * chunk, chunk), view_cols(v)],
                    give_send.at[v, 0], give_recv.at[v, j], sibling, plane,
                ).wait_recv()

    both[pl.ds(0, front), :] = masked[...]
    both[pl.ds(front, front), :] = z_full[...]
    for j in range(width // block):
        depth = pl.ds(j * block, width - j * block)
        here = pl.ds(j * block, block)
        product = dot3(both[:, depth], factor[depth, here])
        stacked[pl.ds(0, front), here] = product[:front]
        out_update[:, here] = -product[front:]
    stacked[pl.ds(front, sep_rows), :] = factor[rows_of(me), :]

    s_cols = s_full.shape[2]
    repeat = n_col * s_cols // width
    my_block = lax.div(plane, repeat)
    my_cols = pl.ds(pl.multiple_of(my_block * s_cols, 128), s_cols)
    stacked_y[pl.ds(0, front), :] = -out_update[:, my_cols]
    stacked_y[pl.ds(front, sep_rows), :] = stacked[pl.ds(front, sep_rows), my_cols]
    right = halves(stacked_y[...])
    split = 128 // sep_rows
    for j in range(width // 128):
        left = halves(stacked[:, pl.ds(j * 128, 128)].T)
        product = dot_pieces(left, right)
        for i in range(split):
            q = j * split + i
            s_part[q % 2, q // 2] = product[i * sep_rows:(i + 1) * sep_rows]
    s_pairing = remote(s_part.at[1 - parity], s_pair, s_pair_sem.at[0], s_pair_sem.at[1], sibling, plane)
    s_pairing.start()
    s_pairing.wait()
    s_half[...] = s_part[parity] + s_pair[...]
    s_phase, s_finish, s_drain = sums(s_half, s_in, s_send, s_recv)
    for s in range(bits):
        s_phase(s)

    def first_of_block(c):
        return lax.rem(c, repeat) == 0

    total = s_finish()

    @pl.when(first_of_block(plane))
    def _():
        s_full[my_block] = total

    s_chain = (lambda c: s_full.at[lax.div(c, repeat)]), first_of_block, s_up_send, s_down_send, s_chain_recv
    for d in range(n_col):
        chain_step(*s_chain, d)
    for j in range(width // s_cols):
        out_sep[:, pl.ds(j * s_cols, s_cols)] = s_full[j]

    s_drain()
    chain_drain(*s_chain)
    for v in range(views):
        pair_copy(v).wait_send()
        reductions[v][2]()
        chain_drain(*z_chain(v))
        for c in range(n_col):
            @pl.when(c != place)
            def _():
                give_copy(v, c).wait_send()

    def sent_rows(cols):
        for b in range(bits):
            far_copy(0, b, cols).wait_send()
        own_copy(cols).wait_send()

    by_width(me, sent_rows)


def on_device(parent_sigma, slot_tile, slot_count, panel, sep_factor):
    n_row = lax.axis_size("row")
    n_col = lax.axis_size("col")
    ratio = n_row // n_col
    slot_cap, tile, width = panel.shape[1:]
    front = slot_cap * tile
    sep_rows = sep_factor.shape[0]
    place = jnp.stack([lax.axis_index("row"), lax.axis_index("col")]).astype(jnp.int32)
    vmem = pl.BlockSpec(memory_space=pltpu.VMEM)
    smem = pl.BlockSpec(memory_space=pltpu.SMEM)
    pairs = n_row // 2
    chunk = ratio * front // n_row
    views = VIEWS
    s_cols = max(128, width // n_col)
    masked, part = pl.pallas_call(
        functools.partial(partial_kernel, ratio),
        out_shape=(
            jax.ShapeDtypeStruct((front, width), F32),
            jax.ShapeDtypeStruct((views, 2, pairs, chunk, width // views), F32),
        ),
        in_specs=[smem, smem, smem, pl.BlockSpec(memory_space=pl.ANY), vmem],
        out_specs=(vmem, vmem),
        scratch_shapes=[
            pltpu.VMEM((ratio * slot_cap, front, tile), F32),
            pltpu.SemaphoreType.DMA((ratio * slot_cap, slot_cap)),
        ],
        compiler_params=pltpu.CompilerParams(vmem_limit_bytes=VMEM_BYTES),
    )(place, slot_tile, slot_count, parent_sigma, panel)

    dma = pltpu.SemaphoreType.DMA
    update, sep = pl.pallas_call(
        functools.partial(main_kernel, n_row, n_col),
        out_shape=(
            jax.ShapeDtypeStruct((front, width), F32),
            jax.ShapeDtypeStruct((sep_rows, width), F32),
        ),
        in_specs=[vmem] * 3,
        out_specs=(vmem, vmem),
        scratch_shapes=[
            pltpu.VMEM((views, pairs, chunk, width // views), F32),
            pltpu.VMEM((views, pairs, chunk, width // views), F32),
            pltpu.VMEM((views, pairs - 1, chunk, width // views), F32),
            pltpu.VMEM((views, n_col, chunk, width // views), F32),
            pltpu.VMEM((front, width), F32),
            pltpu.VMEM((width, width), F32),
            pltpu.VMEM((sep_rows, width), F32),
            pltpu.VMEM((2 * front, width), F32),
            pltpu.VMEM((front + sep_rows, width), F32),
            pltpu.VMEM((front + sep_rows, s_cols), F32),
            pltpu.VMEM((2, pairs, sep_rows, s_cols), F32),
            pltpu.VMEM((pairs, sep_rows, s_cols), F32),
            pltpu.VMEM((pairs, sep_rows, s_cols), F32),
            pltpu.VMEM((pairs - 1, sep_rows, s_cols), F32),
            pltpu.VMEM((width // s_cols, sep_rows, s_cols), F32),
            dma((views,)), dma((views,)), dma((views, pairs - 1)), dma((views, pairs - 1)),
            dma((1,)), dma((1,)), dma((2 * pairs,)), dma((pairs - 1,)), dma((pairs - 1,)), dma((pairs - 1,)),
            dma((views, n_col)), dma((views, n_col)), dma((views, n_col)),
            dma((views, n_col)), dma((views, n_col)),
            dma((2,)), dma((pairs - 1,)), dma((pairs - 1,)), dma((n_col,)), dma((n_col,)), dma((n_col,)),
        ],
        compiler_params=pltpu.CompilerParams(
            collective_id=0, has_side_effects=True, vmem_limit_bytes=VMEM_BYTES
        ),
    )(part, masked, sep_factor)
    return update.reshape(1, slot_cap, tile, width), sep


def solution(mesh):
    placed = (
        P(None, "row", None, None, "col", None),
        P(),
        P(),
        P("row", None, None, None),
        P("row", None),
    )
    return jax.shard_map(
        on_device,
        mesh=mesh,
        in_specs=placed,
        out_specs=(P("row", None, None, None), P("row", None)),
        check_vma=False,
    )
```

time: 93.2 us -> 85.5 us (0.917)
  Pallas kernels: 87.1 us -> 79.5 us
    pallas_call x1, Pallas kernels: 82.4 us -> 74.7 us  [on_device(): pl.pallas_call(functools.partial(main_kernel, n_row, n_col), out_shape=(j...]
where the time goes in v2:
time: 85.5 us; the launch traced here: 85.2 us
  Pallas kernels  79.5 us (93%)
  local copies, waits for them, and re-layouts  4.51 us (5%)
    pallas_call x1, Pallas kernels, on_device(): pl.pallas_call(functools.partial(main_kernel, n_row, n_col), out_shape=(j...  74.7 us
    pallas_call x1, Pallas kernels, on_device(): pl.pallas_call(functools.partial(partial_kernel, ratio), out_shape=(jax.S...  4.74 us
    unnamed x5, local copies, waits for them, and re-layouts  4.51 us

profile of v2, /device:TPU:0, one launch (start us, length us, event | category | flops | bytes accessed | tf_op | source)
XLA Modules:
  0.0 85.2 jit_solution(6235792953184440637)
XLA Ops:
  0.6 0.6 pad_add_fusion.place
  1.2 1.3 %copy.7.tiles = s32[8,2]{1,0:T(8,128)} copy(s32[8,2]{0,1:T(2,128)} %param.6) | data formatting | bytes 128 | tf_op args[1]
  2.5 4.7 %shard_map.68 = (f32[256,1024]{1,0:T(8,128)}, f32[2,2,4,64,512]{4,3,2,1,0:T(8,128)}) custom-call(s32[2]{0:T(128)} %pad_add_fusion.place, s32[8,2]{1,0:T(8,128)} %copy.7.tiles, s32[8]{0:T(128)} %counts.1, f32[4,1,128,8,1,128]{5,4,3,2,1,0:T(1,128)} %sigma.1, f32[1,2,128,1024]{3,2,1,0:T(8,128)} %panel.1), custom_call_target="tpu_custom_call" | custom-call | tf_op jit(solution)/shard_map/pallas_call | solution.py:440
  7.3 74.7 %shard_map.69 = (f32[256,1024]{1,0:T(8,128)}, f32[128,1024]{1,0:T(8,128)}) custom-call(f32[2,2,4,64,512]{4,3,2,1,0:T(8,128)} %get-tuple-element.6.part, f32[256,1024]{1,0:T(8,128)} %get-tuple-element.7.masked, f32[128,1024]{1,0:T(8,128)} %sep.1), custom_call_target="tpu_custom_call" | custom-call | tf_op jit(solution)/shard_map/pallas_call | solution.py:456
  82.0 0.0 copy-start
  82.0 2.4 %copy.10 = f32[1,2,128,1024]{3,2,1,0:T(8,128)} copy(f32[1,2,128,1024]{3,2,1,0:T(8,128)} %bitcast.3) | data formatting | bytes 2097152
  84.4 0.0 copy-done
  84.4 0.8 copy.11
Async XLA Ops:
  82.0 2.4 %copy-start = (f32[128,1024]{1,0:T(8,128)S(1)}, f32[128,1024]{1,0:T(8,128)}, u32[]{:S(2)}) copy-start(f32[128,1024]{1,0:T(8,128)} %get-tuple-element.13) | copy-start | bytes 1572868

commit v3 on v2

--- a/solution.py
+++ b/solution.py
@@ -31,42 +31,6 @@
 
 def exact(left, right):
     return jnp.dot(left, right, precision=lax.Precision.HIGHEST, preferred_element_type=F32)
-
-
-def partial_kernel(ratio, place, tiles, counts, sigma, panel, masked, part, picked, sems):
-    slot_cap, tile, _ = panel.shape[1:]
-    my_row, my_col = place[0], place[1]
-    n_col = tiles.shape[0] // ratio
-    copies = []
-    for k in range(ratio * slot_cap):
-        step, slot = divmod(k, slot_cap)
-        column = tiles[my_col + n_col * step, slot] * ratio + step
-        for s in range(slot_cap):
-            copy = pltpu.make_async_copy(
-                sigma.at[tiles[my_row, s], 0, :, column, 0, :],
-                picked.at[k, pl.ds(s * tile, tile)],
-                sems.at[k, s],
-            )
-            copy.start()
-            copies.append(copy)
-    for s in range(slot_cap):
-        live = jnp.where(s < counts[my_row], 1.0, 0.0).astype(F32)
-        masked[pl.ds(s * tile, tile), :] = panel[0, s] * live
-    strips = halves(masked[...])
-    for copy in copies:
-        copy.wait()
-    for k in range(ratio * slot_cap):
-        step, slot = divmod(k, slot_cap)
-        live = jnp.where(slot < counts[my_col + n_col * step], 1.0, 0.0).astype(F32)
-        block = picked[k].T * live
-        product = dot_pieces(halves(block), strips)
-        views, _, _, chunk, view_width = part.shape
-        for i in range(tile // chunk):
-            q = k * (tile // chunk) + i
-            for v in range(views):
-                part[v, q % 2, q // 2] = product[
-                    i * chunk:(i + 1) * chunk, v * view_width:(v + 1) * view_width
-                ]
 
 
 def base_inverse(block):
@@ -83,13 +47,14 @@
 
 
 def main_kernel(
-    n_row, n_col, part, masked, sep, out_update, out_sep,
-    pair_in, half_sum, scatter_in, chain, z_full, factor, own_rows, both, stacked, stacked_y,
+    n_row, n_col, tiles, counts, sigma, panel, sep, out_update, out_sep,
+    part, pair_in, half_sum, scatter_in, chain, z_full, factor, own_rows,
+    strips_high, strips_low, inverse_high, inverse_low, left_high, left_low, stacked, stacked_y,
     s_part, s_pair, s_half, s_in, s_full,
     pair_send, pair_recv, scatter_send, scatter_recv,
     own_send, own_recv, far_send, far_recv, pass_send, pass_recv,
     up_send, down_send, chain_recv, give_send, give_recv,
-    s_pair_sem, s_send, s_recv, s_up_send, s_down_send, s_chain_recv,
+    s_pair_send, s_pair_recv, s_send, s_recv, s_up_send, s_down_send, s_chain_recv,
 ):
     me, plane = lax.axis_index("row"), lax.axis_index("col")
     pairs = n_row // 2
@@ -98,7 +63,10 @@
     sibling = me + 1 - 2 * parity
     width = sep.shape[1]
     sep_rows = sep.shape[0]
-    front = masked.shape[0]
+    slot_cap, tile = panel.shape[1], panel.shape[2]
+    front = slot_cap * tile
+    ratio = n_row // n_col
+    parent_cols = sigma.shape[2]
     chunk = half_sum.shape[2]
     views = half_sum.shape[0]
     view_width = width // views
@@ -159,7 +127,26 @@
     def pair_copy(v):
         return remote(part.at[v, 1 - parity], pair_in.at[v], pair_send.at[v], pair_recv.at[v], sibling, plane)
 
+    for s in range(slot_cap):
+        live = jnp.where(s < counts[me], 1.0, 0.0).astype(F32)
+        rows = pl.ds(s * tile, tile)
+        strips_high[rows, :], strips_low[rows, :] = halves(panel[0, s] * live)
+    picked = []
+    for k in range(ratio * slot_cap):
+        step, slot = divmod(k, slot_cap)
+        owner = plane + n_col * step
+        column = tiles[owner, slot] * ratio + step
+        live = jnp.where(slot < counts[owner], 1.0, 0.0).astype(F32)
+        stored = [sigma[tiles[me, s], :, column, :] for s in range(slot_cap)]
+        picked.append(halves(jnp.concatenate(stored, axis=0).T * live))
     for v in range(views):
+        here = pl.ds(v * view_width, view_width)
+        right = strips_high[:, here], strips_low[:, here]
+        for k in range(ratio * slot_cap):
+            product = dot_pieces(picked[k], right)
+            for i in range(tile // chunk):
+                q = k * (tile // chunk) + i
+                part[v, q % 2, q // 2] = product[i * chunk:(i + 1) * chunk]
         pair_copy(v).start()
     block = 256
     for g in range(width // block - 1):
@@ -306,7 +293,46 @@
     def z_chain(v):
         return functools.partial(lambda v, c: chain.at[v, c], v), always, up_send.at[v], down_send.at[v], chain_recv.at[v]
 
+    def invert():
+        by_width(sibling, lambda cols: own_copy(cols).wait_recv())
+        for offset in range(1, pairs):
+            by_width(row_block(offset) + 1 - 2 * parity, lambda cols: pass_copy(offset, cols).wait_recv())
+
+            def sent(cols):
+                for b in range(offset.bit_length(), bits):
+                    far_copy(offset, b, cols).wait_send()
+                pass_copy(offset, cols).wait_send()
+
+            by_width(row_block(offset), sent)
+        if not whole_tile:
+            for j in range(width // 128):
+                tile = pl.ds(j * 128, 128)
+                factor[tile, tile] = base_inverse(factor[tile, tile])
+        size = max(sep_rows, 128) if whole_tile else 128
+        while size < width:
+            for start in range(0, width, 2 * size):
+                first, last = pl.ds(start, size), pl.ds(start + size, size)
+                inner = dot3(factor[last, first], factor[first, first])
+                factor[last, first] = -dot3(factor[last, last], inner)
+            size *= 2
+
+        for j in range(width // block):
+            depth = pl.ds(j * block, width - j * block)
+            here = pl.ds(j * block, block)
+            inverse_high[depth, here], inverse_low[depth, here] = halves(factor[depth, here])
+            stacked[pl.ds(0, front), here] = dot_pieces(
+                (strips_high[:, depth], strips_low[:, depth]), (inverse_high[depth, here], inverse_low[depth, here])
+            )
+        stacked[pl.ds(front, sep_rows), :] = factor[rows_of(me), :]
+        for j in range(width // 128):
+            rows = pl.ds(j * 128, 128)
+            left_high[rows, :], left_low[rows, :] = halves(stacked[:, rows].T)
+
     for d in range(n_col):
+        if d == n_col - 1:
+            for offset in range(n_col, pairs):
+                forward_rows(offset)
+            invert()
         for v in range(views):
             if d == 0:
                 chain[v, plane] = reductions[v][1]()
@@ -321,32 +347,8 @@
                 def _():
                     give(v, plane + d)
 
-        if d + 1 < pairs:
+        if d + 1 < min(n_col, pairs):
             forward_rows(d + 1)
-    for offset in range(n_col + 1, pairs):
-        forward_rows(offset)
-
-    by_width(sibling, lambda cols: own_copy(cols).wait_recv())
-    for offset in range(1, pairs):
-        by_width(row_block(offset) + 1 - 2 * parity, lambda cols: pass_copy(offset, cols).wait_recv())
-
-        def sent(cols):
-            for b in range(offset.bit_length(), bits):
-                far_copy(offset, b, cols).wait_send()
-            pass_copy(offset, cols).wait_send()
-
-        by_width(row_block(offset), sent)
-    if not whole_tile:
-        for j in range(width // 128):
-            tile = pl.ds(j * 128, 128)
-            factor[tile, tile] = base_inverse(factor[tile, tile])
-    size = max(sep_rows, 128) if whole_tile else 128
-    while size < width:
-        for start in range(0, width, 2 * size):
-            first, last = pl.ds(start, size), pl.ds(start + size, size)
-            inner = dot3(factor[last, first], factor[first, first])
-            factor[last, first] = -dot3(factor[last, last], inner)
-        size *= 2
 
     for j in range(n_col):
         @pl.when(j != place)
@@ -357,17 +359,15 @@
                     give_send.at[v, 0], give_recv.at[v, j], sibling, plane,
                 ).wait_recv()
 
-    both[pl.ds(0, front), :] = masked[...]
-    both[pl.ds(front, front), :] = z_full[...]
+    z_pieces = halves(z_full[...])
     for j in range(width // block):
-        depth = pl.ds(j * block, width - j * block)
-        here = pl.ds(j * block, block)
-        product = dot3(both[:, depth], factor[depth, here])
-        stacked[pl.ds(0, front), here] = product[:front]
-        out_update[:, here] = -product[front:]
-    stacked[pl.ds(front, sep_rows), :] = factor[rows_of(me), :]
-
-    s_cols = s_full.shape[2]
+        depth, here = slice(j * block, width), pl.ds(j * block, block)
+        out_update[:, here] = -dot_pieces(
+            tuple(piece[:, depth] for piece in z_pieces), (inverse_high[depth, here], inverse_low[depth, here])
+        )
+
+    s_views, s_width = s_full.shape[0], s_full.shape[3]
+    s_cols = s_views * s_width
     repeat = n_col * s_cols // width
     my_block = lax.div(plane, repeat)
     my_cols = pl.ds(pl.multiple_of(my_block * s_cols, 128), s_cols)
@@ -376,36 +376,55 @@
     right = halves(stacked_y[...])
     split = 128 // sep_rows
     for j in range(width // 128):
-        left = halves(stacked[:, pl.ds(j * 128, 128)].T)
-        product = dot_pieces(left, right)
+        rows = pl.ds(j * 128, 128)
+        product = dot_pieces((left_high[rows, :], left_low[rows, :]), right)
         for i in range(split):
             q = j * split + i
-            s_part[q % 2, q // 2] = product[i * sep_rows:(i + 1) * sep_rows]
-    s_pairing = remote(s_part.at[1 - parity], s_pair, s_pair_sem.at[0], s_pair_sem.at[1], sibling, plane)
-    s_pairing.start()
-    s_pairing.wait()
-    s_half[...] = s_part[parity] + s_pair[...]
-    s_phase, s_finish, s_drain = sums(s_half, s_in, s_send, s_recv)
-    for s in range(bits):
-        s_phase(s)
+            for v in range(s_views):
+                s_part[v, q % 2, q // 2] = product[
+                    i * sep_rows:(i + 1) * sep_rows, v * s_width:(v + 1) * s_width
+                ]
+
+    def s_pair_copy(v):
+        return remote(s_part.at[v, 1 - parity], s_pair.at[v], s_pair_send.at[v], s_pair_recv.at[v], sibling, plane)
 
     def first_of_block(c):
         return lax.rem(c, repeat) == 0
 
-    total = s_finish()
-
-    @pl.when(first_of_block(plane))
-    def _():
-        s_full[my_block] = total
-
-    s_chain = (lambda c: s_full.at[lax.div(c, repeat)]), first_of_block, s_up_send, s_down_send, s_chain_recv
+    def s_chain(v):
+        return (
+            functools.partial(lambda v, c: s_full.at[v, lax.div(c, repeat)], v), first_of_block,
+            s_up_send.at[v], s_down_send.at[v], s_chain_recv.at[v],
+        )
+
+    s_sums = [sums(s_half.at[v], s_in.at[v], s_send.at[v], s_recv.at[v]) for v in range(s_views)]
+    for v in range(s_views):
+        s_pair_copy(v).start()
+    for v in range(s_views):
+        s_pair_copy(v).wait_recv()
+        s_half[v] = s_part[v, parity] + s_pair[v]
+        s_sums[v][0](0)
+    for s in range(1, bits):
+        for v in range(s_views):
+            s_sums[v][0](s)
     for d in range(n_col):
-        chain_step(*s_chain, d)
+        for v in range(s_views):
+            if d == 0:
+                total = s_sums[v][1]()
+
+                @pl.when(first_of_block(plane))
+                def _():
+                    s_full[v, my_block] = total
+
+            chain_step(*s_chain(v), d)
     for j in range(width // s_cols):
-        out_sep[:, pl.ds(j * s_cols, s_cols)] = s_full[j]
-
-    s_drain()
-    chain_drain(*s_chain)
+        for v in range(s_views):
+            out_sep[:, pl.ds(j * s_cols + v * s_width, s_width)] = s_full[v, j]
+
+    for v in range(s_views):
+        s_pair_copy(v).wait_send()
+        s_sums[v][2]()
+        chain_drain(*s_chain(v))
     for v in range(views):
         pair_copy(v).wait_send()
         reductions[v][2]()
@@ -430,28 +449,17 @@
     slot_cap, tile, width = panel.shape[1:]
     front = slot_cap * tile
     sep_rows = sep_factor.shape[0]
-    place = jnp.stack([lax.axis_index("row"), lax.axis_index("col")]).astype(jnp.int32)
     vmem = pl.BlockSpec(memory_space=pltpu.VMEM)
     smem = pl.BlockSpec(memory_space=pltpu.SMEM)
     pairs = n_row // 2
     chunk = ratio * front // n_row
     views = VIEWS
     s_cols = max(128, width // n_col)
-    masked, part = pl.pallas_call(
-        functools.partial(partial_kernel, ratio),
-        out_shape=(
-            jax.ShapeDtypeStruct((front, width), F32),
-            jax.ShapeDtypeStruct((views, 2, pairs, chunk, width // views), F32),
-        ),
-        in_specs=[smem, smem, smem, pl.BlockSpec(memory_space=pl.ANY), vmem],
-        out_specs=(vmem, vmem),
-        scratch_shapes=[
-            pltpu.VMEM((ratio * slot_cap, front, tile), F32),
-            pltpu.SemaphoreType.DMA((ratio * slot_cap, slot_cap)),
-        ],
-        compiler_params=pltpu.CompilerParams(vmem_limit_bytes=VMEM_BYTES),
-    )(place, slot_tile, slot_count, parent_sigma, panel)
-
+    s_views = 2 if s_cols % 256 == 0 else 1
+    parts = (views, pairs, chunk, width // views)
+    s_parts = (s_views, pairs, sep_rows, s_cols // s_views)
+    parent_rows, _, _, parent_cols = parent_sigma.shape[:4]
+    sigma = parent_sigma.reshape(parent_rows, tile, parent_cols, tile)
     dma = pltpu.SemaphoreType.DMA
     update, sep = pl.pallas_call(
         functools.partial(main_kernel, n_row, n_col),
@@ -459,34 +467,41 @@
             jax.ShapeDtypeStruct((front, width), F32),
             jax.ShapeDtypeStruct((sep_rows, width), F32),
         ),
-        in_specs=[vmem] * 3,
+        in_specs=[smem, smem, vmem, vmem, vmem],
         out_specs=(vmem, vmem),
         scratch_shapes=[
-            pltpu.VMEM((views, pairs, chunk, width // views), F32),
-            pltpu.VMEM((views, pairs, chunk, width // views), F32),
-            pltpu.VMEM((views, pairs - 1, chunk, width // views), F32),
-            pltpu.VMEM((views, n_col, chunk, width // views), F32),
+            pltpu.VMEM((views, 2) + parts[1:], F32),
+            pltpu.VMEM(parts, F32),
+            pltpu.VMEM(parts, F32),
+            pltpu.VMEM((views, pairs - 1) + parts[2:], F32),
+            pltpu.VMEM((views, n_col) + parts[2:], F32),
             pltpu.VMEM((front, width), F32),
             pltpu.VMEM((width, width), F32),
             pltpu.VMEM((sep_rows, width), F32),
-            pltpu.VMEM((2 * front, width), F32),
+            pltpu.VMEM((front, width), BF16),
+            pltpu.VMEM((front, width), BF16),
+            pltpu.VMEM((width, width), BF16),
+            pltpu.VMEM((width, width), BF16),
+            pltpu.VMEM((width, front + sep_rows), BF16),
+            pltpu.VMEM((width, front + sep_rows), BF16),
             pltpu.VMEM((front + sep_rows, width), F32),
             pltpu.VMEM((front + sep_rows, s_cols), F32),
-            pltpu.VMEM((2, pairs, sep_rows, s_cols), F32),
-            pltpu.VMEM((pairs, sep_rows, s_cols), F32),
-            pltpu.VMEM((pairs, sep_rows, s_cols), F32),
-            pltpu.VMEM((pairs - 1, sep_rows, s_cols), F32),
-            pltpu.VMEM((width // s_cols, sep_rows, s_cols), F32),
+            pltpu.VMEM((s_views, 2) + s_parts[1:], F32),
+            pltpu.VMEM(s_parts, F32),
+            pltpu.VMEM(s_parts, F32),
+            pltpu.VMEM((s_views, pairs - 1) + s_parts[2:], F32),
+            pltpu.VMEM((s_views, width // s_cols) + s_parts[2:], F32),
             dma((views,)), dma((views,)), dma((views, pairs - 1)), dma((views, pairs - 1)),
             dma((1,)), dma((1,)), dma((2 * pairs,)), dma((pairs - 1,)), dma((pairs - 1,)), dma((pairs - 1,)),
             dma((views, n_col)), dma((views, n_col)), dma((views, n_col)),
             dma((views, n_col)), dma((views, n_col)),
-            dma((2,)), dma((pairs - 1,)), dma((pairs - 1,)), dma((n_col,)), dma((n_col,)), dma((n_col,)),
+            dma((s_views,)), dma((s_views,)), dma((s_views, pairs - 1)), dma((s_views, pairs - 1)),
+            dma((s_views, n_col)), dma((s_views, n_col)), dma((s_views, n_col)),
         ],
         compiler_params=pltpu.CompilerParams(
             collective_id=0, has_side_effects=True, vmem_limit_bytes=VMEM_BYTES
         ),
-    )(part, masked, sep_factor)
+    )(slot_tile, slot_count, sigma, panel, sep_factor)
     return update.reshape(1, slot_cap, tile, width), sep
 
 

time: 85.5 us -> 83 us (0.971)
  Pallas kernels: 79.5 us -> 77 us
    pallas_call x1 -> x0, Pallas kernels: 4.74 us -> none  [on_device(): pl.pallas_call(functools.partial(partial_kernel, ratio), out_shape=(jax.S...]
    pallas_call x1, Pallas kernels: 74.7 us -> 77 us  [on_device(): pl.pallas_call(functools.partial(main_kernel, n_row, n_col), out_shape=(j...]
where the time goes in v3:
time: 83 us; the launch traced here: 82.1 us
  Pallas kernels  77 us (93%)
  local copies, waits for them, and re-layouts  4.51 us (5%)
    pallas_call x1, Pallas kernels, on_device(): pl.pallas_call(functools.partial(main_kernel, n_row, n_col), out_shape=(j...  77 us
    unnamed x5, local copies, waits for them, and re-layouts  4.51 us

profile of v3, /device:TPU:0, one launch (start us, length us, event | category | flops | bytes accessed | tf_op | source)
XLA Modules:
  0.0 82.1 jit_solution(11158115098927175795)
XLA Ops:
  0.6 1.3 %copy.7.tiles = s32[8,2]{1,0:T(8,128)} copy(s32[8,2]{0,1:T(2,128)} %param.6) | data formatting | bytes 128 | tf_op args[1]
  2.0 77.0 %shard_map.68 = (f32[256,1024]{1,0:T(8,128)}, f32[128,1024]{1,0:T(8,128)}) custom-call(s32[8,2]{1,0:T(8,128)} %copy.7.tiles, s32[8]{0:T(128)} %counts.1, f32[4,128,8,128]{3,2,1,0:T(8,128)} %bitcast.2, f32[1,2,128,1024]{3,2,1,0:T(8,128)} %panel.1, f32[128,1024]{1,0:T(8,128)} %sep.1), custom_call_target="tpu_custom_call" | custom-call | tf_op jit(solution)/shard_map/pallas_call | solution.py:464
  78.9 0.0 copy-start
  78.9 2.4 %copy.10 = f32[1,2,128,1024]{3,2,1,0:T(8,128)} copy(f32[1,2,128,1024]{3,2,1,0:T(8,128)} %bitcast.3) | data formatting | bytes 2097152
  81.3 0.0 copy-done
  81.3 0.8 copy.11
Async XLA Ops:
  78.9 2.4 %copy-start = (f32[128,1024]{1,0:T(8,128)S(1)}, f32[128,1024]{1,0:T(8,128)}, u32[]{:S(2)}) copy-start(f32[128,1024]{1,0:T(8,128)} %get-tuple-element.9) | copy-start | bytes 1572868

commit v4 on v3

--- a/solution.py
+++ b/solution.py
@@ -27,10 +27,6 @@
 
 def dot3(left, right):
     return dot_pieces(halves(left), halves(right))
-
-
-def exact(left, right):
-    return jnp.dot(left, right, precision=lax.Precision.HIGHEST, preferred_element_type=F32)
 
 
 def base_inverse(block):
@@ -42,17 +38,17 @@
     for level in range(size.bit_length() - 1):
         row_block, col_block = row >> level, col >> level
         below = jnp.where((row_block == col_block + 1) & ((row_block & 1) == 1), block, 0.0)
-        inverse = inverse - exact(inverse, exact(below, inverse))
+        inverse = inverse - dot3(inverse, dot3(below, inverse))
     return inverse
 
 
 def main_kernel(
     n_row, n_col, tiles, counts, sigma, panel, sep, out_update, out_sep,
-    part, pair_in, half_sum, scatter_in, chain, z_full, factor, own_rows,
+    part, pair_in, half_sum, scatter_in, chain, z_full, factor, diagonals,
     strips_high, strips_low, inverse_high, inverse_low, left_high, left_low, stacked, stacked_y,
     s_part, s_pair, s_half, s_in, s_full,
     pair_send, pair_recv, scatter_send, scatter_recv,
-    own_send, own_recv, far_send, far_recv, pass_send, pass_recv,
+    own_send, own_recv, far_send, far_recv, pass_send, pass_recv, tile_send, tile_recv,
     up_send, down_send, chain_recv, give_send, give_recv,
     s_pair_send, s_pair_recv, s_send, s_recv, s_up_send, s_down_send, s_chain_recv,
 ):
@@ -124,6 +120,80 @@
 
         return phase, finish, drain
 
+    block = 256
+    other_order = order[::-1]
+
+    def rows_of(q):
+        return pl.ds(pl.multiple_of(q * sep_rows, 8), sep_rows)
+
+    def by_width(q, action):
+        for g in range(width // block):
+            @pl.when(lax.div(q * sep_rows, block) == g)
+            def _():
+                action(pl.ds(0, (g + 1) * block))
+
+    def row_block(offset):
+        return 2 * moved(order, offset) + parity
+
+    def sibling_block(offset):
+        return 2 * moved(other_order, offset) + 1 - parity
+
+    def own_copy(cols):
+        return remote(sep.at[:, cols], factor.at[rows_of(me), cols], own_send.at[0], own_recv.at[0], sibling, plane)
+
+    def far_copy(offset, b, cols):
+        rows = rows_of(row_block(offset))
+        source = factor.at[rows, cols] if offset else sep.at[:, cols]
+        slot = offset + (1 << b) - 1
+        return remote(
+            source, factor.at[rows, cols], far_send.at[slot], far_recv.at[slot],
+            2 * (mine + order[b]) + parity, plane,
+        )
+
+    def arrived(offset, cols):
+        b = offset.bit_length() - 1
+        rows = rows_of(row_block(offset))
+        remote(
+            factor.at[rows, cols], factor.at[rows, cols], far_send.at[offset - 1], far_recv.at[offset - 1],
+            2 * (mine + order[b]) + parity, plane,
+        ).wait_recv()
+
+    def pass_copy(q, offset, cols):
+        rows = rows_of(q)
+        return remote(
+            factor.at[rows, cols], factor.at[rows, cols],
+            pass_send.at[offset - 1], pass_recv.at[offset - 1], sibling, plane,
+        )
+
+    def start_rest(cols):
+        for b in range(1, bits):
+            far_copy(0, b, cols).start()
+        own_copy(cols).start()
+        factor[rows_of(me), cols] = sep[:, cols]
+
+    def forward_rows(offset):
+        def action(cols):
+            arrived(offset, cols)
+            for b in range(offset.bit_length(), bits):
+                far_copy(offset, b, cols).start()
+            pass_copy(row_block(offset), offset, cols).start()
+
+        by_width(row_block(offset), action)
+
+    def tile_own():
+        return remote(diagonals.at[me], diagonals.at[me], tile_send.at[0], tile_recv.at[0], sibling, plane)
+
+    def tile_far(offset):
+        return remote(
+            diagonals.at[me], diagonals.at[me], tile_send.at[offset], tile_recv.at[offset], row_block(offset), plane
+        )
+
+    def tile_pass(q, offset):
+        slot = pairs - 1 + offset
+        return remote(diagonals.at[q], diagonals.at[q], tile_send.at[slot], tile_recv.at[slot], sibling, plane)
+
+    by_width(me, lambda cols: far_copy(0, 0, cols).start())
+
     def pair_copy(v):
         return remote(part.at[v, 1 - parity], pair_in.at[v], pair_send.at[v], pair_recv.at[v], sibling, plane)
 
@@ -135,9 +205,9 @@
     for k in range(ratio * slot_cap):
         step, slot = divmod(k, slot_cap)
         owner = plane + n_col * step
-        column = tiles[owner, slot] * ratio + step
+        column = tiles[slot, owner] * ratio + step
         live = jnp.where(slot < counts[owner], 1.0, 0.0).astype(F32)
-        stored = [sigma[tiles[me, s], :, column, :] for s in range(slot_cap)]
+        stored = [sigma[tiles[s, me], :, column, :] for s in range(slot_cap)]
         picked.append(halves(jnp.concatenate(stored, axis=0).T * live))
     for v in range(views):
         here = pl.ds(v * view_width, view_width)
@@ -148,7 +218,6 @@
                 q = k * (tile // chunk) + i
                 part[v, q % 2, q // 2] = product[i * chunk:(i + 1) * chunk]
         pair_copy(v).start()
-    block = 256
     for g in range(width // block - 1):
         rest = width - (g + 1) * block
         factor[pl.ds(g * block, block), pl.ds((g + 1) * block, rest)] = jnp.zeros((block, rest), F32)
@@ -160,72 +229,16 @@
         half_sum[v] = part[v, parity] + pair_in[v]
         reductions[v][0](0)
 
-    own_rows[...] = sep[...]
     whole_tile = sep_rows % 128 == 0
     if whole_tile:
-        diagonal = pl.ds(pl.multiple_of(me * sep_rows, 128), sep_rows)
-        own_rows[:, diagonal] = base_inverse(sep[:, diagonal])
+        diagonals[me] = base_inverse(sep[:, pl.ds(pl.multiple_of(me * sep_rows, 128), sep_rows)])
+        tile_own().start()
+        for offset in range(1, pairs):
+            tile_far(offset).start()
     for s in range(1, bits):
         for v in range(views):
             reductions[v][0](s)
-
-    def rows_of(q):
-        return pl.ds(pl.multiple_of(q * sep_rows, 8), sep_rows)
-
-    def by_width(q, action):
-        for g in range(width // block):
-            @pl.when(lax.div(q * sep_rows, block) == g)
-            def _():
-                action(pl.ds(0, (g + 1) * block))
-
-    def row_block(offset):
-        return 2 * moved(flip, offset) + parity
-
-    def own_copy(cols):
-        return remote(
-            own_rows.at[:, cols], factor.at[rows_of(me), cols], own_send.at[0], own_recv.at[0], sibling, plane
-        )
-
-    def far_copy(offset, b, cols):
-        rows = rows_of(row_block(offset))
-        source = factor.at[rows, cols] if offset else own_rows.at[:, cols]
-        slot = offset + (1 << b) - 1
-        return remote(
-            source, factor.at[rows, cols], far_send.at[slot], far_recv.at[slot],
-            2 * (mine + flip[b]) + parity, plane,
-        )
-
-    def arrived(offset, cols):
-        b = offset.bit_length() - 1
-        rows = rows_of(row_block(offset))
-        remote(
-            factor.at[rows, cols], factor.at[rows, cols], far_send.at[offset - 1], far_recv.at[offset - 1],
-            2 * (mine + flip[b]) + parity, plane,
-        ).wait_recv()
-
-    def pass_copy(offset, cols):
-        rows = rows_of(row_block(offset))
-        return remote(
-            factor.at[rows, cols], factor.at[rows, cols],
-            pass_send.at[offset - 1], pass_recv.at[offset - 1], sibling, plane,
-        )
-
-    def start_rows(cols):
-        for b in range(bits):
-            far_copy(0, b, cols).start()
-        own_copy(cols).start()
-        factor[rows_of(me), cols] = own_rows[:, cols]
-
-    by_width(me, start_rows)
-
-    def forward_rows(offset):
-        def action(cols):
-            arrived(offset, cols)
-            for b in range(offset.bit_length(), bits):
-                far_copy(offset, b, cols).start()
-            pass_copy(offset, cols).start()
-
-        by_width(row_block(offset), action)
+    by_width(me, start_rest)
 
     owner_step = lax.div(me, n_col)
     place = lax.rem(me, n_col)
@@ -294,17 +307,30 @@
         return functools.partial(lambda v, c: chain.at[v, c], v), always, up_send.at[v], down_send.at[v], chain_recv.at[v]
 
     def invert():
+        if whole_tile:
+            for offset in range(1, pairs):
+                tile_far(offset).wait_recv()
+                tile_pass(row_block(offset), offset).start()
         by_width(sibling, lambda cols: own_copy(cols).wait_recv())
         for offset in range(1, pairs):
-            by_width(row_block(offset) + 1 - 2 * parity, lambda cols: pass_copy(offset, cols).wait_recv())
+            by_width(
+                sibling_block(offset), lambda cols: pass_copy(sibling_block(offset), offset, cols).wait_recv()
+            )
 
             def sent(cols):
                 for b in range(offset.bit_length(), bits):
                     far_copy(offset, b, cols).wait_send()
-                pass_copy(offset, cols).wait_send()
+                pass_copy(row_block(offset), offset, cols).wait_send()
 
             by_width(row_block(offset), sent)
-        if not whole_tile:
+        if whole_tile:
+            tile_own().wait_recv()
+            for offset in range(1, pairs):
+                tile_pass(sibling_block(offset), offset).wait_recv()
+            for q in range(n_row):
+                tile_at = pl.ds(q * sep_rows, sep_rows)
+                factor[tile_at, tile_at] = diagonals[q]
+        else:
             for j in range(width // 128):
                 tile = pl.ds(j * 128, 128)
                 factor[tile, tile] = base_inverse(factor[tile, tile])
@@ -440,6 +466,25 @@
         own_copy(cols).wait_send()
 
     by_width(me, sent_rows)
+    if whole_tile:
+        tile_own().wait_send()
+        for offset in range(1, pairs):
+            tile_far(offset).wait_send()
+            tile_pass(row_block(offset), offset).wait_send()
+
+
+def hand_over(update, sep, update_out, sep_out, sems):
+    parts = 4
+    copies = []
+    for i, (source, target) in enumerate(((update, update_out), (sep, sep_out))):
+        rows = source.shape[0] // parts
+        for j in range(parts):
+            here = pl.ds(j * rows, rows)
+            copy = pltpu.make_async_copy(source.at[here], target.at[here], sems.at[i, j])
+            copy.start()
+            copies.append(copy)
+    for copy in copies:
+        copy.wait()
 
 
 def on_device(parent_sigma, slot_tile, slot_count, panel, sep_factor):
@@ -477,7 +522,7 @@
             pltpu.VMEM((views, n_col) + parts[2:], F32),
             pltpu.VMEM((front, width), F32),
             pltpu.VMEM((width, width), F32),
-            pltpu.VMEM((sep_rows, width), F32),
+            pltpu.VMEM((n_row, sep_rows, sep_rows), F32),
             pltpu.VMEM((front, width), BF16),
             pltpu.VMEM((front, width), BF16),
             pltpu.VMEM((width, width), BF16),
@@ -493,6 +538,7 @@
             pltpu.VMEM((s_views, width // s_cols) + s_parts[2:], F32),
             dma((views,)), dma((views,)), dma((views, pairs - 1)), dma((views, pairs - 1)),
             dma((1,)), dma((1,)), dma((2 * pairs,)), dma((pairs - 1,)), dma((pairs - 1,)), dma((pairs - 1,)),
+            dma((2 * pairs - 1,)), dma((2 * pairs - 1,)),
             dma((views, n_col)), dma((views, n_col)), dma((views, n_col)),
             dma((views, n_col)), dma((views, n_col)),
             dma((s_views,)), dma((s_views,)), dma((s_views, pairs - 1)), dma((s_views, pairs - 1)),
@@ -501,7 +547,18 @@
         compiler_params=pltpu.CompilerParams(
             collective_id=0, has_side_effects=True, vmem_limit_bytes=VMEM_BYTES
         ),
-    )(slot_tile, slot_count, sigma, panel, sep_factor)
+    )(slot_tile.T, slot_count, sigma, panel, sep_factor)
+    anywhere = pl.BlockSpec(memory_space=pl.ANY)
+    update, sep = pl.pallas_call(
+        hand_over,
+        out_shape=(
+            jax.ShapeDtypeStruct((front, width), F32),
+            jax.ShapeDtypeStruct((sep_rows, width), F32),
+        ),
+        in_specs=[anywhere] * 2,
+        out_specs=(anywhere, anywhere),
+        scratch_shapes=[dma((2, 4))],
+    )(update, sep)
     return update.reshape(1, slot_cap, tile, width), sep
 
 

time: 83 us -> 130 us (1.57)
  Pallas kernels: 77 us -> 129 us
  local copies, waits for them, and re-layouts: 4.51 us -> 0 us
    pallas_call x0 -> x1, Pallas kernels: none -> 48.8 us  [on_device(): pl.pallas_call(hand_over, out_shape=(jax.ShapeDtypeStruct((front, width),...]
    unnamed x5 -> x0, local copies, waits for them, and re-layouts: 4.51 us -> none
    pallas_call x1, Pallas kernels: 77 us -> 80 us  [on_device(): pl.pallas_call(functools.partial(main_kernel, n_row, n_col), out_shape=(j...]
where the time goes in v4:
time: 130 us
  Pallas kernels  129 us (99%)
    pallas_call x1, Pallas kernels, on_device(): pl.pallas_call(functools.partial(main_kernel, n_row, n_col), out_shape=(j...  80 us
    pallas_call x1, Pallas kernels, on_device(): pl.pallas_call(hand_over, out_shape=(jax.ShapeDtypeStruct((front, width),...  48.8 us

profile of v4, /device:TPU:0, one launch (start us, length us, event | category | flops | bytes accessed | tf_op | source)
XLA Modules:
  0.0 129.5 jit_solution(7652517963081280389)
XLA Ops:
  0.6 80.0 %shard_map.68 = (f32[256,1024]{1,0:T(8,128)}, f32[128,1024]{1,0:T(8,128)}) custom-call(s32[2,8]{1,0:T(2,128)} %bitcast.4, s32[8]{0:T(128)} %counts.1, f32[4,128,8,128]{3,2,1,0:T(8,128)} %bitcast.3, f32[1,2,128,1024]{3,2,1,0:T(8,128)} %panel.1, f32[128,1024]{1,0:T(8,128)} %sep.1), custom_call_target="tpu_custom_call" | custom-call | tf_op jit(solution)/shard_map/pallas_call | solution.py:509
  80.7 48.8 %shard_map.69 = (f32[256,1024]{1,0:T(8,128)}, f32[128,1024]{1,0:T(8,128)}) custom-call(f32[256,1024]{1,0:T(8,128)} %get-tuple-element.6.update, f32[128,1024]{1,0:T(8,128)} %get-tuple-element.7.sep), custom_call_target="tpu_custom_call" | custom-call | tf_op jit(solution)/shard_map/pallas_call | solution.py:552

commit v5 on v4

--- a/solution.py
+++ b/solution.py
@@ -11,7 +11,7 @@
 F32 = jnp.float32
 BF16 = jnp.bfloat16
 VMEM_BYTES = 56 * 1024 * 1024
-VIEWS = 2
+VIEWS = 4
 
 
 def halves(x):
@@ -21,8 +21,9 @@
 
 def dot_pieces(left, right):
     (lh, ll), (rh, rl) = left, right
-    one = functools.partial(jnp.dot, preferred_element_type=F32)
-    return one(lh, rh) + (one(lh, rl) + one(ll, rh))
+    rows = lh.shape[0]
+    both = jnp.dot(jnp.concatenate([lh, ll], axis=0), rh, preferred_element_type=F32)
+    return both[:rows] + (both[rows:] + jnp.dot(lh, rl, preferred_element_type=F32))
 
 
 def dot3(left, right):
@@ -45,7 +46,7 @@
 def main_kernel(
     n_row, n_col, tiles, counts, sigma, panel, sep, out_update, out_sep,
     part, pair_in, half_sum, scatter_in, chain, z_full, factor, diagonals,
-    strips_high, strips_low, inverse_high, inverse_low, left_high, left_low, stacked, stacked_y,
+    strips_high, strips_low, picked_high, picked_low, inverse_high, inverse_low, left_high, left_low, stacked, stacked_y,
     s_part, s_pair, s_half, s_in, s_full,
     pair_send, pair_recv, scatter_send, scatter_recv,
     own_send, own_recv, far_send, far_recv, pass_send, pass_recv, tile_send, tile_recv,
@@ -201,23 +202,30 @@
         live = jnp.where(s < counts[me], 1.0, 0.0).astype(F32)
         rows = pl.ds(s * tile, tile)
         strips_high[rows, :], strips_low[rows, :] = halves(panel[0, s] * live)
-    picked = []
     for k in range(ratio * slot_cap):
         step, slot = divmod(k, slot_cap)
         owner = plane + n_col * step
         column = tiles[slot, owner] * ratio + step
         live = jnp.where(slot < counts[owner], 1.0, 0.0).astype(F32)
         stored = [sigma[tiles[s, me], :, column, :] for s in range(slot_cap)]
-        picked.append(halves(jnp.concatenate(stored, axis=0).T * live))
+        high, low = halves(jnp.concatenate(stored, axis=0).T * live)
+        for i in range(tile // chunk):
+            q = k * (tile // chunk) + i
+            here, rows = pl.ds(q // 2 * chunk, chunk), slice(i * chunk, (i + 1) * chunk)
+            picked_high[q % 2, here], picked_low[q % 2, here] = high[rows], low[rows]
+
+    def multiply(side, v):
+        here = pl.ds(v * view_width, view_width)
+        product = dot_pieces(
+            (picked_high[side], picked_low[side]), (strips_high[:, here], strips_low[:, here])
+        )
+        part[v, side] = product.reshape(pairs, chunk, view_width)
+
     for v in range(views):
-        here = pl.ds(v * view_width, view_width)
-        right = strips_high[:, here], strips_low[:, here]
-        for k in range(ratio * slot_cap):
-            product = dot_pieces(picked[k], right)
-            for i in range(tile // chunk):
-                q = k * (tile // chunk) + i
-                part[v, q % 2, q // 2] = product[i * chunk:(i + 1) * chunk]
+        multiply(1 - parity, v)
         pair_copy(v).start()
+    for v in range(views):
+        multiply(parity, v)
     for g in range(width // block - 1):
         rest = width - (g + 1) * block
         factor[pl.ds(g * block, block), pl.ds((g + 1) * block, rest)] = jnp.zeros((block, rest), F32)
@@ -229,16 +237,18 @@
         half_sum[v] = part[v, parity] + pair_in[v]
         reductions[v][0](0)
 
+    for s in range(1, bits):
+        for v in range(views):
+            reductions[v][0](s)
+    by_width(me, start_rest)
+
     whole_tile = sep_rows % 128 == 0
-    if whole_tile:
+
+    def send_tile():
         diagonals[me] = base_inverse(sep[:, pl.ds(pl.multiple_of(me * sep_rows, 128), sep_rows)])
         tile_own().start()
         for offset in range(1, pairs):
             tile_far(offset).start()
-    for s in range(1, bits):
-        for v in range(views):
-            reductions[v][0](s)
-    by_width(me, start_rest)
 
     owner_step = lax.div(me, n_col)
     place = lax.rem(me, n_col)
@@ -350,13 +360,17 @@
                 (strips_high[:, depth], strips_low[:, depth]), (inverse_high[depth, here], inverse_low[depth, here])
             )
         stacked[pl.ds(front, sep_rows), :] = factor[rows_of(me), :]
+        split = 128 // sep_rows
         for j in range(width // 128):
-            rows = pl.ds(j * 128, 128)
-            left_high[rows, :], left_low[rows, :] = halves(stacked[:, rows].T)
+            high, low = halves(stacked[:, pl.ds(j * 128, 128)].T)
+            for i in range(split):
+                q = j * split + i
+                rows, here = slice(i * sep_rows, (i + 1) * sep_rows), pl.ds(q // 2 * sep_rows, sep_rows)
+                left_high[q % 2, here], left_low[q % 2, here] = high[rows], low[rows]
 
     for d in range(n_col):
         if d == n_col - 1:
-            for offset in range(n_col, pairs):
+            for offset in range(2, pairs):
                 forward_rows(offset)
             invert()
         for v in range(views):
@@ -373,8 +387,10 @@
                 def _():
                     give(v, plane + d)
 
-        if d + 1 < min(n_col, pairs):
-            forward_rows(d + 1)
+        if d == 0:
+            forward_rows(1)
+            if whole_tile:
+                send_tile()
 
     for j in range(n_col):
         @pl.when(j != place)
@@ -400,16 +416,11 @@
     stacked_y[pl.ds(0, front), :] = -out_update[:, my_cols]
     stacked_y[pl.ds(front, sep_rows), :] = stacked[pl.ds(front, sep_rows), my_cols]
     right = halves(stacked_y[...])
-    split = 128 // sep_rows
-    for j in range(width // 128):
-        rows = pl.ds(j * 128, 128)
-        product = dot_pieces((left_high[rows, :], left_low[rows, :]), right)
-        for i in range(split):
-            q = j * split + i
-            for v in range(s_views):
-                s_part[v, q % 2, q // 2] = product[
-                    i * sep_rows:(i + 1) * sep_rows, v * s_width:(v + 1) * s_width
-                ]
+    def s_multiply(side):
+        product = dot_pieces((left_high[side], left_low[side]), right)
+        for v in range(s_views):
+            here = slice(v * s_width, (v + 1) * s_width)
+            s_part[v, side] = product[:, here].reshape(pairs, sep_rows, s_width)
 
     def s_pair_copy(v):
         return remote(s_part.at[v, 1 - parity], s_pair.at[v], s_pair_send.at[v], s_pair_recv.at[v], sibling, plane)
@@ -424,8 +435,10 @@
         )
 
     s_sums = [sums(s_half.at[v], s_in.at[v], s_send.at[v], s_recv.at[v]) for v in range(s_views)]
+    s_multiply(1 - parity)
     for v in range(s_views):
         s_pair_copy(v).start()
+    s_multiply(parity)
     for v in range(s_views):
         s_pair_copy(v).wait_recv()
         s_half[v] = s_part[v, parity] + s_pair[v]
@@ -471,20 +484,6 @@
         for offset in range(1, pairs):
             tile_far(offset).wait_send()
             tile_pass(row_block(offset), offset).wait_send()
-
-
-def hand_over(update, sep, update_out, sep_out, sems):
-    parts = 4
-    copies = []
-    for i, (source, target) in enumerate(((update, update_out), (sep, sep_out))):
-        rows = source.shape[0] // parts
-        for j in range(parts):
-            here = pl.ds(j * rows, rows)
-            copy = pltpu.make_async_copy(source.at[here], target.at[here], sems.at[i, j])
-            copy.start()
-            copies.append(copy)
-    for copy in copies:
-        copy.wait()
 
 
 def on_device(parent_sigma, slot_tile, slot_count, panel, sep_factor):
@@ -525,10 +524,12 @@
             pltpu.VMEM((n_row, sep_rows, sep_rows), F32),
             pltpu.VMEM((front, width), BF16),
             pltpu.VMEM((front, width), BF16),
+            pltpu.VMEM((2, pairs * chunk, front), BF16),
+            pltpu.VMEM((2, pairs * chunk, front), BF16),
             pltpu.VMEM((width, width), BF16),
             pltpu.VMEM((width, width), BF16),
-            pltpu.VMEM((width, front + sep_rows), BF16),
-            pltpu.VMEM((width, front + sep_rows), BF16),
+            pltpu.VMEM((2, width // 2, front + sep_rows), BF16),
+            pltpu.VMEM((2, width // 2, front + sep_rows), BF16),
             pltpu.VMEM((front + sep_rows, width), F32),
             pltpu.VMEM((front + sep_rows, s_cols), F32),
             pltpu.VMEM((s_views, 2) + s_parts[1:], F32),
@@ -548,17 +549,6 @@
             collective_id=0, has_side_effects=True, vmem_limit_bytes=VMEM_BYTES
         ),
     )(slot_tile.T, slot_count, sigma, panel, sep_factor)
-    anywhere = pl.BlockSpec(memory_space=pl.ANY)
-    update, sep = pl.pallas_call(
-        hand_over,
-        out_shape=(
-            jax.ShapeDtypeStruct((front, width), F32),
-            jax.ShapeDtypeStruct((sep_rows, width), F32),
-        ),
-        in_specs=[anywhere] * 2,
-        out_specs=(anywhere, anywhere),
-        scratch_shapes=[dma((2, 4))],
-    )(update, sep)
     return update.reshape(1, slot_cap, tile, width), sep
 
 

time: 130 us -> 83 us (0.64)
  Pallas kernels: 129 us -> 79 us
  local copies, waits for them, and re-layouts: 0 us -> 3.16 us
    pallas_call x1 -> x0, Pallas kernels: 48.8 us -> none  [on_device(): pl.pallas_call(hand_over, out_shape=(jax.ShapeDtypeStruct((front, width),...]
    unnamed x0 -> x4, local copies, waits for them, and re-layouts: none -> 3.16 us
where the time goes in v5:
time: 83 us; the launch traced here: 82.8 us
  Pallas kernels  79 us (95%)
  local copies, waits for them, and re-layouts  3.16 us (4%)
    pallas_call x1, Pallas kernels, on_device(): pl.pallas_call(functools.partial(main_kernel, n_row, n_col), out_shape=(j...  79 us
    unnamed x4, local copies, waits for them, and re-layouts  3.16 us

profile of v5, /device:TPU:0, one launch (start us, length us, event | category | flops | bytes accessed | tf_op | source)
XLA Modules:
  0.0 82.8 jit_solution(425964140045388881)
XLA Ops:
  0.6 79.0 %shard_map.68 = (f32[256,1024]{1,0:T(8,128)}, f32[128,1024]{1,0:T(8,128)}) custom-call(s32[2,8]{1,0:T(2,128)} %bitcast.5, s32[8]{0:T(128)} %counts.1, f32[4,128,8,128]{3,2,1,0:T(8,128)} %bitcast.3, f32[1,2,128,1024]{3,2,1,0:T(8,128)} %panel.1, f32[128,1024]{1,0:T(8,128)} %sep.1), custom_call_target="tpu_custom_call" | custom-call | tf_op jit(solution)/shard_map/pallas_call | solution.py:508
  79.6 0.0 copy-start
  79.6 2.4 %copy.9 = f32[1,2,128,1024]{3,2,1,0:T(8,128)} copy(f32[1,2,128,1024]{3,2,1,0:T(8,128)} %bitcast.4) | data formatting | bytes 2097152
  82.0 0.0 copy-done
  82.0 0.8 copy.10
Async XLA Ops:
  79.6 2.4 %copy-start = (f32[128,1024]{1,0:T(8,128)S(1)}, f32[128,1024]{1,0:T(8,128)}, u32[]{:S(2)}) copy-start(f32[128,1024]{1,0:T(8,128)} %get-tuple-element.9) | copy-start | bytes 1572868

commit v6 on v5

--- a/solution.py
+++ b/solution.py
@@ -11,7 +11,7 @@
 F32 = jnp.float32
 BF16 = jnp.bfloat16
 VMEM_BYTES = 56 * 1024 * 1024
-VIEWS = 4
+VIEWS = 2
 
 
 def halves(x):
@@ -237,11 +237,6 @@
         half_sum[v] = part[v, parity] + pair_in[v]
         reductions[v][0](0)
 
-    for s in range(1, bits):
-        for v in range(views):
-            reductions[v][0](s)
-    by_width(me, start_rest)
-
     whole_tile = sep_rows % 128 == 0
 
     def send_tile():
@@ -249,6 +244,13 @@
         tile_own().start()
         for offset in range(1, pairs):
             tile_far(offset).start()
+
+    if whole_tile:
+        send_tile()
+    for s in range(1, bits):
+        for v in range(views):
+            reductions[v][0](s)
+    by_width(me, start_rest)
 
     owner_step = lax.div(me, n_col)
     place = lax.rem(me, n_col)
@@ -370,7 +372,7 @@
 
     for d in range(n_col):
         if d == n_col - 1:
-            for offset in range(2, pairs):
+            for offset in range(n_col, pairs):
                 forward_rows(offset)
             invert()
         for v in range(views):
@@ -387,10 +389,8 @@
                 def _():
                     give(v, plane + d)
 
-        if d == 0:
-            forward_rows(1)
-            if whole_tile:
-                send_tile()
+        if d + 1 < min(n_col, pairs):
+            forward_rows(d + 1)
 
     for j in range(n_col):
         @pl.when(j != place)

time: 83 us -> 84.8 us (1.022)
  Pallas kernels: 79 us -> 80.9 us
    pallas_call x1, Pallas kernels: 79 us -> 80.9 us  [on_device(): pl.pallas_call(functools.partial(main_kernel, n_row, n_col), out_shape=(j...]
where the time goes in v6:
time: 84.8 us; the launch traced here: 84.7 us
  Pallas kernels  80.9 us (95%)
  local copies, waits for them, and re-layouts  3.16 us (4%)
    pallas_call x1, Pallas kernels, on_device(): pl.pallas_call(functools.partial(main_kernel, n_row, n_col), out_shape=(j...  80.9 us
    unnamed x4, local copies, waits for them, and re-layouts  3.16 us

profile of v6, /device:TPU:0, one launch (start us, length us, event | category | flops | bytes accessed | tf_op | source)
XLA Modules:
  0.0 84.7 jit_solution(12910357650678029807)
XLA Ops:
  0.6 80.9 %shard_map.68 = (f32[256,1024]{1,0:T(8,128)}, f32[128,1024]{1,0:T(8,128)}) custom-call(s32[2,8]{1,0:T(2,128)} %bitcast.5, s32[8]{0:T(128)} %counts.1, f32[4,128,8,128]{3,2,1,0:T(8,128)} %bitcast.3, f32[1,2,128,1024]{3,2,1,0:T(8,128)} %panel.1, f32[128,1024]{1,0:T(8,128)} %sep.1), custom_call_target="tpu_custom_call" | custom-call | tf_op jit(solution)/shard_map/pallas_call | solution.py:508
  81.5 0.0 copy-start
  81.5 2.4 %copy.9 = f32[1,2,128,1024]{3,2,1,0:T(8,128)} copy(f32[1,2,128,1024]{3,2,1,0:T(8,128)} %bitcast.4) | data formatting | bytes 2097152
  83.9 0.0 copy-done
  83.9 0.8 copy.10
Async XLA Ops:
  81.5 2.4 %copy-start = (f32[128,1024]{1,0:T(8,128)S(1)}, f32[128,1024]{1,0:T(8,128)}, u32[]{:S(2)}) copy-start(f32[128,1024]{1,0:T(8,128)} %get-tuple-element.9) | copy-start | bytes 1572868
